TPU v7x, 128 devices: a whole 4x4x4 slice. The times are simulated.
128 devices in a mesh: gx: 16 (over x, z), gy: 8 (over y, core).
Axes of the slice: x: 4, y: 4, z: 4, core: 2. Of those that a mesh axis runs over, the one named last changes fastest.
Arguments:
- layer_slowness: float32 [8], replicated, may hold values from 0.5 to 2
- layer_rigidity: float32 [8], replicated, may hold values from 0.5 to 4
- layer_damping: float32 [8], replicated, may hold values from 0.02 to 0.2
- layer_of_level: int32 [32], replicated, may hold values from 0 to 7
- slot_offset: int32 [32768], replicated, may hold values from 0 to 2047
- slot_level: int32 [32768], replicated, may hold values from 0 to 31
- slot_target: int32 [32768], P(('gx', 'gy')), may hold values from 0 to 786431
- live_count: int32 [128], P(('gx', 'gy')), may hold values from 1 to 256, 16384 in all
- moduli: float32 [2, 512, 256, 256], P(None, 'gx', 'gy'), may hold values from 0.02 to 0.06
- field_old: float32 [3, 512, 256, 256], P(None, 'gx', 'gy'), may hold values from -0.3 to 0.3
- field_now: float32 [3, 512, 256, 256], P(None, 'gx', 'gy'), may hold values from -0.3 to 0.3
Outputs:
- final_field: float32 [3, 512, 256, 256], P(None, 'gx', 'gy')
- prior_field: float32 [3, 512, 256, 256], P(None, 'gx', 'gy')
Inputs may be any that keep to these rules, and one draw needn't show every extreme that they name: live_count sums to 32768 // 2 over all owners, and some owner uses all 256 slots.
All inputs are finite; a program needn't handle non-finite values. No bound on the sum of `live_count` on one device may be relied on, other than what follows from the above.
Results may differ from a plain program's by a relative error of at most 0.0036.
Values may be sent and summed in bfloat16 or wider, within the bound.
A program may use at most 128 MiB of HBM per device.

v0:
```python
import functools
import math

import jax
import jax.numpy as jnp
import ml_dtypes
import numpy as np
from jax import lax
from jax.experimental import pallas as pl
from jax.experimental.pallas import tpu as pltpu
from jax.sharding import PartitionSpec as P

F = 128
NK = 1024
NR = 2048
ND = 32
STEPS = 4
TSTART = 32
GX = 16
GY = 8
C = 32
NZ = 256
Q = 256
GROUPS = 8
XG = 4
ROWS = XG * C
LINKS = 8
MESH = pl.DeviceIdType.MESH
BF = jnp.bfloat16
F32 = jnp.float32


def constants():
    y2 = np.zeros((ROWS, ROWS + 32), np.float32)
    y1 = np.zeros((ROWS, ROWS + 32), np.float32)
    low, high = ROWS, ROWS + 16

    def place(x, y):
        if y < 0:
            return low + 2 * (x + 1) + y + 2
        if y >= C:
            return high + 2 * (x + 1) + y - C
        return x * C + y

    for x in range(XG):
        for y in range(C):
            row = x * C + y
            for shift, factor in ((-2, -1.0), (-1, 16.0), (0, -30.0), (1, 16.0), (2, -1.0)):
                y2[row, place(x, y + shift)] += factor
            y1[row, place(x, y + 1)] += 1.0
            y1[row, place(x, y - 1)] -= 1.0
    cross = np.zeros((3, ROWS, ROWS + 96), np.float32)
    for kind in range(3):
        cross[kind, :, :ROWS] = 3.0 * y1[:, :ROWS]
        cross[kind, :, ROWS + 64 :] = 3.0 * y1[:, ROWS:]
        for x in range(XG):
            for y, beyond, sign in ((0, -1, -3.0), (C - 1, C, 3.0)):
                for step in (-1, 1):
                    outside = (kind == 0 and x + step < 0) or (kind == 2 and x + step >= XG)
                    if outside:
                        spot = ROWS + 32 + 15 if beyond < 0 else ROWS + 48
                    else:
                        spot = place(x + step, beyond)
                    cross[kind, x * C + y, spot] += sign * step
    pick = np.zeros((3, 32, 6 * C), np.float32)
    for kind in range(3):
        for i in range(6):
            x = i - 1 + kind if kind != 1 else i
            if kind == 0:
                x = i - 1
            elif kind == 2:
                x = i + 1
            if 0 <= x < 6:
                for k in range(2):
                    pick[kind, 2 * i + k, x * C + C - 2 + k] = 1.0
                    pick[kind, 16 + 2 * i + k, x * C + k] = 1.0
    z2 = np.zeros((NZ, NZ), np.float32)
    z1 = np.zeros((NZ, NZ), np.float32)
    for z in range(NZ):
        for shift, factor in ((-2, -1.0), (-1, 16.0), (0, -30.0), (1, 16.0), (2, -1.0)):
            if 0 <= z + shift < NZ:
                z2[z + shift, z] += factor
        if z + 1 < NZ:
            z1[z + 1, z] += 1.0
        if z > 0:
            z1[z - 1, z] -= 1.0
    period = 2 * F
    turns = (np.arange(F)[None, :] + 1) * (TSTART + np.arange(STEPS)[:, None]) % period
    angles = turns * (2.0 * math.pi / period)
    weight = 1.0 / math.sqrt(F)
    waves = np.concatenate([weight * np.cos(angles), -weight * np.sin(angles)], axis=1).T
    waves = np.repeat(waves.astype(np.float32), ND, axis=1)
    upper = waves.astype(ml_dtypes.bfloat16)
    lower = (waves - upper.astype(np.float32)).astype(ml_dtypes.bfloat16)
    ones = np.zeros((STEPS, STEPS * ND, NZ), np.float32)
    for n in range(STEPS):
        ones[n, n * ND : (n + 1) * ND] = 1.0
    half = ml_dtypes.bfloat16
    return dict(
        y2=y2.astype(half),
        y1=y1.astype(half),
        cross=cross.astype(half),
        pick=pick.astype(half),
        z2=z2.astype(half),
        z1=z1.astype(half),
        z3=(3.0 * z1).astype(half),
        waves=np.concatenate([upper, lower], axis=1),
        ones=ones.astype(half),
    )


def dot(a, b):
    return jnp.dot(a, b, preferred_element_type=F32)


def advance(window, lows, highs, clows, chighs, now, before, lam, mu, sources, y2, y1, cross, z2, z1, z3):
    wide = [w.astype(F32) for w in window]
    inner = [w[2 : 2 + XG].reshape(ROWS, NZ) for w in window]
    second = [
        (16.0 * (w[1:5] + w[3:7]) - (w[0:4] + w[4:8]) - 30.0 * w[2:6]).reshape(ROWS, NZ)
        for w in wide
    ]
    first = [(w[3:7] - w[1:5]).reshape(ROWS, NZ) for w in wide]
    ends = [jnp.concatenate([lows[c], highs[c]], axis=0) for c in range(3)]
    tall = [jnp.concatenate([inner[c], ends[c]], axis=0) for c in range(3)]
    along_y = [dot(y2, tall[c]) for c in range(3)]
    along_z = [dot(inner[c], z2) for c in range(3)]
    skew_z = dot(tall[2], z1)
    skew_y = dot(y1, tall[1])
    mix_0 = dot(
        cross[:, : ROWS + 64],
        jnp.concatenate([first[1].astype(BF), ends[1], clows[1], chighs[1]], axis=0),
    ) + dot(first[2].astype(BF), z3)
    mix_1 = dot(
        cross,
        jnp.concatenate(
            [
                (first[0] + skew_z[:ROWS]).astype(BF),
                ends[0],
                clows[0],
                chighs[0],
                skew_z[ROWS:].astype(BF),
            ],
            axis=0,
        ),
    )
    mix_2 = dot((first[0] + skew_y).astype(BF), z3)
    couple = [second[0] + mix_0, along_y[1] + mix_1, along_z[2] + mix_2]
    joint = lam + mu
    result = []
    for c in range(3):
        lap = second[c] + (along_y[c] + along_z[c])
        moved = (mu * lap + joint * couple[c]) * (1.0 / 12.0)
        result.append((2.0 * now[c] - before[c]) + (moved + sources[c]))
    return result


def sine(x):
    y = x * x
    poly = -2.5052108e-08
    for coefficient in (2.7557319e-06, -1.9841270e-04, 8.3333333e-03, -1.6666667e-01, 1.0):
        poly = poly * y + coefficient
    return x * poly


def cosine(x):
    y = x * x
    poly = -2.7557319e-07
    for coefficient in (2.4801587e-05, -1.3888889e-03, 4.1666667e-02, -0.5, 1.0):
        poly = poly * y + coefficient
    return poly


def lane_spread(row):
    return jnp.transpose(jnp.broadcast_to(row.astype(F32), (128, 128))).astype(jnp.int32)


def main_kernel(
    slow_ref, rigid_ref, damp_ref, level_ref, live_ref, target_ref,
    y2_ref, y1_ref, cross_ref, pick_ref, z2_ref, z1_ref, z3_ref, waves_ref, ones_ref,
    offsets_hbm, levels_hbm, moduli_hbm, old_hbm, now_hbm,
    last_hbm, prior_hbm, half_hbm, side_hbm, corner_hbm, spread_hbm,
    field, mod, half, side_out, side_in, corner, hot, gathered, basis, spread,
    slot_tile, zbuf, ebuf, dbuf, kbuf,
    load_sem, store_sem, send_sem, recv_sem, gsend_sem, grecv_sem,
):
    gx = lax.axis_index("gx")
    gy = lax.axis_index("gy")
    device = gx * GY + gy
    px, pz = gx // 4, gx % 4
    py, core = gy // 2, gy % 2
    block = core * 64 + px * 16 + pz * 4 + py

    loads = [
        pltpu.make_async_copy(now_hbm, field.at[0], load_sem.at[0]),
        pltpu.make_async_copy(old_hbm, field.at[1], load_sem.at[1]),
        pltpu.make_async_copy(moduli_hbm, mod, load_sem.at[2]),
        pltpu.make_async_copy(
            offsets_hbm.at[pl.ds(pl.multiple_of(device // 4 * 8, 8), 8)], slot_tile.at[0], load_sem.at[3]
        ),
        pltpu.make_async_copy(
            levels_hbm.at[pl.ds(pl.multiple_of(device // 4 * 8, 8), 8)], slot_tile.at[1], load_sem.at[4]
        ),
    ]
    for load in loads:
        load.start()

    for p in range(2):
        half[p, :, 0:2] = jnp.zeros((3, 2, C, NZ), BF)
        half[p, :, C + 2 : C + 4] = jnp.zeros((3, 2, C, NZ), BF)
        corner[p] = jnp.zeros(corner.shape[1:], BF)
        for s in range(2):
            side_in[p, s] = jnp.zeros(side_in.shape[2:], BF)

    steps = [(1, 0), (-1, 0), (0, 1), (0, -1), (1, 1), (1, -1), (-1, 1), (-1, -1)]

    def exists(dx, dy):
        ok = None
        for delta, place, size in ((dx, gx, GX), (dy, gy, GY)):
            if delta == 1:
                part = place < size - 1
            elif delta == -1:
                part = place > 0
            else:
                continue
            ok = part if ok is None else jnp.logical_and(ok, part)
        return ok

    barrier = pltpu.get_barrier_semaphore()
    for dx, dy in steps:
        @pl.when(exists(dx, dy))
        def _():
            pl.semaphore_signal(barrier, inc=1, device_id=(gx + dx, gy + dy), device_id_type=MESH)

    def ring_y(k):
        return (gx, (py + k) % 4 * 2 + core)

    def ring_z(k):
        return (px * 4 + (pz + k) % 4, gy)

    def ring_x(k):
        return ((px + k) % 4 * 4 + pz, gy)

    for ring in (ring_y, ring_z, ring_x):
        for k in (1, 2, 3):
            pl.semaphore_signal(barrier, inc=1, device_id=ring(k), device_id_type=MESH)
    twin = (gx, py * 2 + 1 - core)
    pl.semaphore_signal(barrier, inc=1, device_id=twin, device_id_type=MESH)

    rows = lax.broadcasted_iota(jnp.int32, (8, 128), 0) + block * 8
    wavenum = (rows.astype(F32) + 0.5) * (4.0 / NK)
    square_k = wavenum * wavenum
    omega = (lax.broadcasted_iota(jnp.int32, (8, 128), 1) + 1).astype(F32) * (4.0 / F)

    def downward(i, carry):
        down_re, down_im = carry
        layer = level_ref[i]
        part = omega * slow_ref[layer]
        vertical = jnp.sqrt(square_k + part * part)
        fade = jnp.exp(vertical * (-0.25 * damp_ref[layer]))
        angle = 0.125 * vertical
        s, c = sine(angle), cosine(angle)
        leg_re = fade * (1.0 - 2.0 * s * s)
        leg_im = fade * (-2.0 * s * c)
        zbuf[i] = rigid_ref[layer] * vertical
        ebuf[0, i] = leg_re
        ebuf[1, i] = leg_im
        dbuf[0, i] = down_re
        dbuf[1, i] = down_im
        return down_re * leg_re - down_im * leg_im, down_re * leg_im + down_im * leg_re

    one = jnp.ones((8, 128), F32)
    zero = jnp.zeros((8, 128), F32)
    lax.fori_loop(0, ND, downward, (one, zero), unroll=4)
    zbuf[ND] = zbuf[ND - 1]

    def upward(step, carry):
        refl_re, refl_im = carry
        i = ND - 1 - step
        upper, under = zbuf[i], zbuf[i + 1]
        r = (upper - under) / (upper + under)
        leg_re, leg_im = ebuf[0, i], ebuf[1, i]
        trip_re = leg_re * leg_re - leg_im * leg_im
        trip_im = 2.0 * leg_re * leg_im
        upper_re = r + refl_re
        lower_re = 1.0 + r * refl_re
        lower_im = r * refl_im
        scale = 1.0 / (lower_re * lower_re + lower_im * lower_im)
        ratio_re = (upper_re * lower_re + refl_im * lower_im) * scale
        ratio_im = (refl_im * lower_re - upper_re * lower_im) * scale
        fresh_re = trip_re * ratio_re - trip_im * ratio_im
        fresh_im = trip_re * ratio_im + trip_im * ratio_re
        down_re, down_im = dbuf[0, i], dbuf[1, i]
        kbuf[i, :, 0:128] = (down_re * (1.0 + fresh_re) - down_im * fresh_im) * (1.0 / 32.0)
        kbuf[i, :, 128:256] = (down_re * fresh_im + down_im * (1.0 + fresh_re)) * (1.0 / 32.0)
        return fresh_re, fresh_im

    lax.fori_loop(0, ND, upward, (zero, zero), unroll=4)
    product = dot(kbuf[...].reshape(ND * 8, 2 * F).astype(BF), waves_ref[...])
    product = product[:, :128] + product[:, 128:]
    lane = lax.broadcasted_iota(jnp.int32, (8, 128), 1) % ND
    mine = zero
    for d in range(ND):
        mine = jnp.where(lane == d, product[8 * d : 8 * d + 8], mine)
    gathered[block] = mine

    count = 10
    for dx, dy in steps:
        count = count + exists(dx, dy).astype(jnp.int32)
    pl.semaphore_wait(barrier, count)

    def stage(index, ring, start, size):
        copies = []
        for k in (1, 2, 3):
            piece = gathered.at[pl.ds(start, size)]
            copies.append(
                pltpu.make_async_remote_copy(
                    src_ref=piece,
                    dst_ref=piece,
                    send_sem=gsend_sem.at[3 * index + k - 1],
                    recv_sem=grecv_sem.at[3 * index + k - 1],
                    device_id=ring(k),
                    device_id_type=MESH,
                )
            )
        for copy in copies:
            copy.start()
        return copies

    def finish(copies):
        for copy in copies:
            copy.wait()

    stage_y = stage(0, ring_y, block, 1)

    def to_half(g, carry):
        x = g * XG
        for c in range(3):
            half[0, c, pl.ds(x + 2, XG)] = field[0, c, pl.ds(x, XG)].astype(BF)
        return carry

    def kind_of(g):
        return (g + GROUPS - 2) // (GROUPS - 1)

    def exchange(n):
        p = n % 2

        def fill(g, carry):
            kind = jnp.where(g == 0, 0, jnp.where(g == GROUPS - 1, 2, 1))
            x = jnp.where(g == 0, 0, jnp.where(g == GROUPS - 1, C - 6, g * XG - 1))
            for c in range(3):
                tile = dot(pick_ref[kind], half[p, c, pl.ds(x + 2, 6)].reshape(6 * C, NZ)).astype(BF)
                side_out[p, 0, c, g] = tile[:16]
                side_out[p, 1, c, g] = tile[16:]
            return carry

        lax.fori_loop(0, GROUPS, fill, 0)
        pairs = [
            (half.at[p, :, pl.ds(C, 2)], half.at[p, :, pl.ds(0, 2)]),
            (half.at[p, :, pl.ds(2, 2)], half.at[p, :, pl.ds(C + 2, 2)]),
            (side_out.at[p, 0], side_in.at[p, 0]),
            (side_out.at[p, 1], side_in.at[p, 1]),
            (half.at[p, pl.ds(0, 2), C + 1, pl.ds(16, 16)], corner.at[p, 0, 0]),
            (half.at[p, pl.ds(0, 2), C + 1, pl.ds(0, 16)], corner.at[p, 0, 1]),
            (half.at[p, pl.ds(0, 2), 2, pl.ds(16, 16)], corner.at[p, 1, 0]),
            (half.at[p, pl.ds(0, 2), 2, pl.ds(0, 16)], corner.at[p, 1, 1]),
        ]
        copies = []
        for index, ((dx, dy), (source, target)) in enumerate(zip(steps, pairs)):
            copies.append(
                pltpu.make_async_remote_copy(
                    src_ref=source,
                    dst_ref=target,
                    send_sem=send_sem.at[n, index],
                    recv_sem=recv_sem.at[n, index],
                    device_id=(gx + dx, gy + dy),
                    device_id_type=MESH,
                )
            )
        for (dx, dy), copy in zip(steps, copies):
            @pl.when(exists(dx, dy))
            def _():
                copy.start()

        return copies

    def settle(copies):
        for (dx, dy), copy in zip(steps, copies):
            @pl.when(exists(dx, dy))
            def _():
                copy.wait_send()

            @pl.when(exists(-dx, -dy))
            def _():
                copy.wait_recv()

    loads[0].wait()
    lax.fori_loop(0, GROUPS, to_half, 0)
    copies = exchange(0)
    finish(stage_y)
    stage_z = stage(1, ring_z, block // 4 * 4, 4)

    loads[3].wait()
    loads[4].wait()
    row = device % 4 * 2
    mask = NK * NR // 2 - 1
    for h in range(2):
        part = pl.ds(128 * h, 128)
        q = lane_spread(slot_tile[0, pl.ds(row + h, 1)])
        lanes = lax.broadcasted_iota(jnp.int32, (128, 128), 1)
        for b in range(NK // 128):
            turns = (2 * (lanes + 128 * b) + 1) * q
            turns = ((turns + (mask + 1) // 2) & mask) - (mask + 1) // 2
            s = sine(turns.astype(F32) * (math.pi / (mask + 1)))
            basis[part, 128 * b : 128 * b + 128] = (1.0 - 2.0 * s * s).astype(BF)
    finish(stage_z)
    stage_x = stage(2, ring_x, block // 16 * 16, 16)

    def build_hot(g, carry):
        ids = lax.broadcasted_iota(jnp.int32, (ROWS, Q), 0) + g * ROWS
        columns = target_ref[...] // NZ
        for c in range(3):
            same = ids + c * C * C == columns
            hot[c, g] = jnp.where(same, 1.0, 0.0).astype(BF)
        return carry

    lax.fori_loop(0, GROUPS, build_hot, 0)
    finish(stage_x)
    whole = gathered.at[pl.ds(core * 64, 64)]
    swap = pltpu.make_async_remote_copy(
        src_ref=whole,
        dst_ref=whole,
        send_sem=gsend_sem.at[9],
        recv_sem=grecv_sem.at[9],
        device_id=twin,
        device_id_type=MESH,
    )
    swap.start()
    swap.wait()

    total = gathered[...].reshape(NK, 128)
    upper = total.astype(BF)
    lower = (total - upper.astype(F32)).astype(BF)
    picked = dot(basis[...], jnp.concatenate([upper, lower], axis=1))
    picked = picked[:, :128] + picked[:, 128:]
    for h in range(2):
        part = slice(128 * h, 128 * h + 128)
        lanes = lax.broadcasted_iota(jnp.int32, (128, 128), 1)
        ids = lax.broadcasted_iota(jnp.int32, (128, 128), 0) + 128 * h
        level = lane_spread(slot_tile[1, pl.ds(row + h, 1)])
        keep = jnp.logical_and(lanes % ND == level, ids < live_ref[0])
        chosen = jnp.where(keep, picked[part], 0.0).astype(BF)
        depth = lane_spread(target_ref[:, 128 * h : 128 * h + 128] % NZ)
        for n in range(STEPS):
            values = dot(chosen, ones_ref[n])
            for b in range(2):
                same = lanes + 128 * b == depth
                spread[n, part, 128 * b : 128 * b + 128] = jnp.where(
                    same, values[:, 128 * b : 128 * b + 128], 0.0
                ).astype(BF)

    loads[1].wait()
    loads[2].wait()
    for n in range(STEPS - 1):
        p = n % 2
        settle(copies)

        def group(g, carry):
            x = g * XG
            kind = jnp.where(g == 0, 0, jnp.where(g == GROUPS - 1, 2, 1))
            right = g // (GROUPS // 2)
            window = [half[p, c, pl.ds(x, XG + 4)] for c in range(3)]
            lows = [side_in[p, 0, c, g] for c in range(3)]
            highs = [side_in[p, 1, c, g] for c in range(3)]
            clows = [corner[p, right, 0, c] for c in range(2)]
            chighs = [corner[p, right, 1, c] for c in range(2)]
            sources = [dot(hot[c, g], spread[n]) for c in range(3)]
            result = advance(
                window, lows, highs, clows, chighs,
                [field[p, c, pl.ds(x, XG)].reshape(ROWS, NZ) for c in range(3)],
                [field[1 - p, c, pl.ds(x, XG)].reshape(ROWS, NZ) for c in range(3)],
                mod[0, pl.ds(x, XG)].reshape(ROWS, NZ),
                mod[1, pl.ds(x, XG)].reshape(ROWS, NZ),
                sources,
                y2_ref[...], y1_ref[...], cross_ref[kind], z2_ref[...], z1_ref[...], z3_ref[...],
            )
            for c in range(3):
                fresh = result[c].reshape(XG, C, NZ)
                field[1 - p, c, pl.ds(x, XG)] = fresh
                half[1 - p, c, pl.ds(x + 2, XG)] = fresh.astype(BF)
            return carry

        lax.fori_loop(0, GROUPS, group, 0)
        copies = exchange(n + 1)

    p = (STEPS - 1) % 2
    stores = [
        pltpu.make_async_copy(field.at[p], last_hbm, store_sem.at[0]),
        pltpu.make_async_copy(field.at[1 - p], prior_hbm, store_sem.at[1]),
        pltpu.make_async_copy(spread.at[STEPS - 1], spread_hbm, store_sem.at[2]),
        pltpu.make_async_copy(half.at[p], half_hbm, store_sem.at[3]),
        pltpu.make_async_copy(side_in.at[p], side_hbm, store_sem.at[4]),
        pltpu.make_async_copy(corner.at[p], corner_hbm, store_sem.at[5]),
    ]
    for store in stores[:3]:
        store.start()
    settle(copies)
    for store in stores[3:]:
        store.start()
    for store in stores:
        store.wait()


def last_kernel(
    target_ref, y2_ref, y1_ref, cross_ref, z2_ref, z1_ref, z3_ref,
    half, side, corner, spread, now_ref, before_ref, mod, final_ref, copy_ref,
):
    g = pl.program_id(0)
    x = g * XG
    kind = jnp.where(g == 0, 0, jnp.where(g == GROUPS - 1, 2, 1))
    right = g // (GROUPS // 2)
    ids = lax.broadcasted_iota(jnp.int32, (ROWS, Q), 0) + g * ROWS
    columns = target_ref[...] // NZ
    sources = [
        dot(jnp.where(ids + c * C * C == columns, 1.0, 0.0).astype(BF), spread[...]) for c in range(3)
    ]
    result = advance(
        [half[c, pl.ds(x, XG + 4)] for c in range(3)],
        [side[0, c, g] for c in range(3)],
        [side[1, c, g] for c in range(3)],
        [corner[right, 0, c] for c in range(2)],
        [corner[right, 1, c] for c in range(2)],
        [now_ref[c].reshape(ROWS, NZ) for c in range(3)],
        [before_ref[c].reshape(ROWS, NZ) for c in range(3)],
        mod[0].reshape(ROWS, NZ),
        mod[1].reshape(ROWS, NZ),
        sources,
        y2_ref[...], y1_ref[...], cross_ref[kind], z2_ref[...], z1_ref[...], z3_ref[...],
    )
    for c in range(3):
        final_ref[c] = result[c].reshape(XG, C, NZ)
        copy_ref[c] = now_ref[c]


def shards(
    layer_slowness, layer_rigidity, layer_damping, layer_of_level,
    slot_offset, slot_level, slot_target, live_count, moduli, field_old, field_now,
):
    fixed = constants()
    smem = pl.BlockSpec(memory_space=pltpu.SMEM)
    vmem = pl.BlockSpec(memory_space=pltpu.VMEM)
    any_space = pl.BlockSpec(memory_space=pl.ANY)
    target = slot_target.reshape(1, Q)
    block = jax.ShapeDtypeStruct((3, C, C, NZ), F32)
    names = ("y2", "y1", "cross", "pick", "z2", "z1", "z3", "waves", "ones")
    dma = pltpu.SemaphoreType.DMA
    last, prior, half, side, corner, spread = pl.pallas_call(
        main_kernel,
        out_shape=[
            block,
            block,
            jax.ShapeDtypeStruct((3, C + 4, C, NZ), BF),
            jax.ShapeDtypeStruct((2, 3, GROUPS, 16, NZ), BF),
            jax.ShapeDtypeStruct((2, 2, 2, 16, NZ), BF),
            jax.ShapeDtypeStruct((Q, NZ), BF),
        ],
        in_specs=[smem] * 5 + [vmem] * (1 + len(names)) + [any_space] * 5,
        out_specs=[any_space] * 6,
        scratch_shapes=[
            pltpu.VMEM((2, 3, C, C, NZ), F32),
            pltpu.VMEM((2, C, C, NZ), F32),
            pltpu.VMEM((2, 3, C + 4, C, NZ), BF),
            pltpu.VMEM((2, 2, 3, GROUPS, 16, NZ), BF),
            pltpu.VMEM((2, 2, 3, GROUPS, 16, NZ), BF),
            pltpu.VMEM((2, 2, 2, 2, 16, NZ), BF),
            pltpu.VMEM((3, GROUPS, ROWS, Q), BF),
            pltpu.VMEM((NK // 8, 8, 128), F32),
            pltpu.VMEM((Q, NK), BF),
            pltpu.VMEM((STEPS, Q, NZ), BF),
            pltpu.VMEM((2, 8, 128), jnp.int32),
            pltpu.VMEM((ND + 1, 8, 128), F32),
            pltpu.VMEM((2, ND, 8, 128), F32),
            pltpu.VMEM((2, ND, 8, 128), F32),
            pltpu.VMEM((ND, 8, 2 * F), F32),
            dma((5,)),
            dma((6,)),
            dma((STEPS, LINKS)),
            dma((STEPS, LINKS)),
            dma((10,)),
            dma((10,)),
        ],
        compiler_params=pltpu.CompilerParams(
            collective_id=0, has_side_effects=True, vmem_limit_bytes=48 * 1024 * 1024
        ),
    )(
        layer_slowness, layer_rigidity, layer_damping, layer_of_level, live_count, target,
        *[jnp.asarray(fixed[name]) for name in names],
        slot_offset.reshape(Q, 128), slot_level.reshape(Q, 128), moduli, field_old, field_now,
    )
    names = ("y2", "y1", "cross", "z2", "z1", "z3")

    def full(shape):
        return pl.BlockSpec(shape, lambda g: (0,) * len(shape))

    rows = pl.BlockSpec((3, XG, C, NZ), lambda g: (0, g, 0, 0))
    matrices = [jnp.asarray(fixed[name]) for name in names]
    return pl.pallas_call(
        last_kernel,
        grid=(GROUPS,),
        out_shape=[block, block],
        in_specs=[full((1, Q))]
        + [full(m.shape) for m in matrices]
        + [full(half.shape), full(side.shape), full(corner.shape), full(spread.shape), rows, rows]
        + [pl.BlockSpec((2, XG, C, NZ), lambda g: (0, g, 0, 0))],
        out_specs=[rows, rows],
        compiler_params=pltpu.CompilerParams(vmem_limit_bytes=48 * 1024 * 1024),
    )(target, *matrices, half, side, corner, spread, last, prior, moduli)


def solution(mesh):
    in_specs = (
        P(),
        P(),
        P(),
        P(),
        P(),
        P(),
        P(("gx", "gy")),
        P(("gx", "gy")),
        P(None, "gx", "gy", None),
        P(None, "gx", "gy", None),
        P(None, "gx", "gy", None),
    )
    out_specs = (P(None, "gx", "gy", None), P(None, "gx", "gy", None))
    return jax.shard_map(shards, mesh=mesh, in_specs=in_specs, out_specs=out_specs, check_vma=False)
```

profile of v0, /device:TPU:3, one launch (start us, length us, event | category | flops | bytes accessed | tf_op | source)
XLA Modules:
  0.0 87.4 jit_solution(16626663389854189368)
XLA Ops:
  1.3 0.0 copy-start
  1.3 1.6 %copy-done = f32[2,32,32,256]{3,2,1,0:T(8,128)S(1)} copy-done((f32[2,32,32,256]{3,2,1,0:T(8,128)S(1)}, f32[2,32,32,256]{3,2,1,0:T(8,128)}, u32[]{:S(2)}) %copy-start) | copy-done | bytes 2097176
  2.9 0.0 copy-start.2
  2.9 0.9 %copy-done.2 = bf16[3,128,224]{2,1,0:T(8,128)(2,1)S(1)} copy-done((bf16[3,128,224]{2,1,0:T(8,128)(2,1)S(1)}, bf16[3,128,224]{2,1,0:T(8,128)(2,1)}, u32[]{:S(2)}) %copy-start.2) | copy-done | bytes 172056
  3.8 0.0 copy-start.4
  3.8 0.9 %copy-done.4 = bf16[256,256]{1,0:T(8,128)(2,1)S(1)} copy-done((bf16[256,256]{1,0:T(8,128)(2,1)S(1)}, bf16[256,256]{1,0:T(8,128)(2,1)}, u32[]{:S(2)}) %copy-start.4) | copy-done | bytes 131096
  4.7 0.0 copy-start.5
  4.7 0.9 %copy-done.5 = bf16[256,256]{1,0:T(8,128)(2,1)S(1)} copy-done((bf16[256,256]{1,0:T(8,128)(2,1)S(1)}, bf16[256,256]{1,0:T(8,128)(2,1)}, u32[]{:S(2)}) %copy-start.5) | copy-done | bytes 131096
  5.6 0.0 copy-start.6
  5.6 0.9 %copy-done.6 = bf16[256,256]{1,0:T(8,128)(2,1)S(1)} copy-done((bf16[256,256]{1,0:T(8,128)(2,1)S(1)}, bf16[256,256]{1,0:T(8,128)(2,1)}, u32[]{:S(2)}) %copy-start.6) | copy-done | bytes 131096
  6.5 0.0 copy-start.7
  6.5 0.8 copy-done.7
  7.4 0.0 copy-start.8
  7.4 0.8 copy-done.8
  8.2 0.0 copy-start.9
  8.2 0.9 %copy-done.9 = bf16[4,128,256]{2,1,0:T(8,128)(2,1)S(1)} copy-done((bf16[4,128,256]{2,1,0:T(8,128)(2,1)S(1)}, bf16[4,128,256]{2,1,0:T(8,128)(2,1)}, u32[]{:S(2)}) %copy-start.9) | copy-done | bytes 262168
  9.1 0.0 copy-start.10
  9.1 0.9 %copy-done.10 = s32[32768]{0:T(1024)S(1)} copy-done((s32[32768]{0:T(1024)S(1)}, s32[32768]{0:T(1024)}, u32[]{:S(2)}) %copy-start.10) | copy-done | bytes 131096
  10.0 0.0 copy-start.11
  10.1 0.9 %copy-done.11 = s32[32768]{0:T(1024)S(1)} copy-done((s32[32768]{0:T(1024)S(1)}, s32[32768]{0:T(1024)}, u32[]{:S(2)}) %copy-start.11) | copy-done | bytes 131096
  11.0 0.0 copy-start.12
  11.0 0.9 %copy-done.12 = bf16[256,256]{1,0:T(8,128)(2,1)S(1)} copy-done((bf16[256,256]{1,0:T(8,128)(2,1)S(1)}, bf16[256,256]{1,0:T(8,128)(2,1)}, u32[]{:S(2)}) %copy-start.12) | copy-done | bytes 131096
  11.9 0.0 copy-start.13
  11.9 0.8 copy-done.13
  12.7 0.0 copy-start.14
  12.7 0.7 copy-done.14
  13.3 0.0 copy-start.15
  13.3 0.7 copy-done.15
  14.0 0.0 copy-start.16
  14.0 0.7 copy-done.16
  14.6 0.0 copy-start.17
  14.6 0.7 copy-done.17
  15.3 0.0 copy-start.18
  15.3 0.7 copy-done.18
  16.0 0.0 copy-start.1
  16.0 0.0 copy-start.3
  16.0 61.8 %shard_map.203 = (f32[3,32,32,256]{3,2,1,0:T(8,128)}, f32[3,32,32,256]{3,2,1,0:T(8,128)}, bf16[3,36,32,256]{3,2,1,0:T(8,128)(2,1)S(1)}, bf16[2,3,8,16,256]{4,3,2...) custom-call(f32[8]{0:T(128)S(1)} %copy-done.15, f32[8]{0:T(128)S(1)} %copy-done.16, ...), custom_call_target="tpu_custom_call" | custom-call | tf_op jit(solution)/shard_map/pallas_call | solution.py:557
  77.7 0.0 copy-done.1
  77.8 0.0 copy-done.3
  77.8 9.7 %shard_map.204 = (f32[3,32,32,256]{3,2,1,0:T(8,128)}, f32[3,32,32,256]{3,2,1,0:T(8,128)}) custom-call(s32[1,256]{1,0:T(1,128)S(1)} %bitcast.6, bf16[128,160]{1,0:T(8,128)(2,1)S(1)} %copy-done.8, bf16[128,160]{1,0:T(8,128)(2,1)S(1)} %copy-done.7, bf16[3,128,224]{2,1,0:T(8,128)(2,1)S(1)} %copy-done.3, bf16[256,256]{1,0:T(8,128)(2,1)S(1)} %copy-done.6, ...), custom_call_target="tpu_custom_call" | custom-call | tf_op jit(solution)/shard_map/pallas_call | solution.py:607
Async XLA Ops:
  1.3 1.6 %copy-start = (f32[2,32,32,256]{3,2,1,0:T(8,128)S(1)}, f32[2,32,32,256]{3,2,1,0:T(8,128)}, u32[]{:S(2)}) copy-start(f32[2,32,32,256]{3,2,1,0:T(8,128)} %mod.1) | copy-start | bytes 6291460
  2.9 0.9 %copy-start.2 = (bf16[3,128,224]{2,1,0:T(8,128)(2,1)S(1)}, bf16[3,128,224]{2,1,0:T(8,128)(2,1)}, u32[]{:S(2)}) copy-start(bf16[3,128,224]{2,1,0:T(8,128)(2,1)} %constant.20.clone.cross_ref) | copy-start | bytes 516100
  3.8 0.9 %copy-start.4 = (bf16[256,256]{1,0:T(8,128)(2,1)S(1)}, bf16[256,256]{1,0:T(8,128)(2,1)}, u32[]{:S(2)}) copy-start(bf16[256,256]{1,0:T(8,128)(2,1)} %constant.24.clone.z3_ref) | copy-start | bytes 393220
  4.7 0.9 %copy-start.5 = (bf16[256,256]{1,0:T(8,128)(2,1)S(1)}, bf16[256,256]{1,0:T(8,128)(2,1)}, u32[]{:S(2)}) copy-start(bf16[256,256]{1,0:T(8,128)(2,1)} %constant.23.clone.z1_ref) | copy-start | bytes 393220
  5.6 0.9 %copy-start.6 = (bf16[256,256]{1,0:T(8,128)(2,1)S(1)}, bf16[256,256]{1,0:T(8,128)(2,1)}, u32[]{:S(2)}) copy-start(bf16[256,256]{1,0:T(8,128)(2,1)} %constant.22.clone.z2_ref) | copy-start | bytes 393220
  6.5 0.8 copy-start.7
  7.4 0.8 copy-start.8
  8.2 0.9 %copy-start.9 = (bf16[4,128,256]{2,1,0:T(8,128)(2,1)S(1)}, bf16[4,128,256]{2,1,0:T(8,128)(2,1)}, u32[]{:S(2)}) copy-start(bf16[4,128,256]{2,1,0:T(8,128)(2,1)} %constant.26.clone.ones_ref) | copy-start | bytes 786436
  9.1 0.9 %copy-start.10 = (s32[32768]{0:T(1024)S(1)}, s32[32768]{0:T(1024)}, u32[]{:S(2)}) copy-start(s32[32768]{0:T(1024)} %param.24) | copy-start | bytes 393220
  10.0 0.9 %copy-start.11 = (s32[32768]{0:T(1024)S(1)}, s32[32768]{0:T(1024)}, u32[]{:S(2)}) copy-start(s32[32768]{0:T(1024)} %param.25) | copy-start | bytes 393220
  11.0 0.9 %copy-start.12 = (bf16[256,256]{1,0:T(8,128)(2,1)S(1)}, bf16[256,256]{1,0:T(8,128)(2,1)}, u32[]{:S(2)}) copy-start(bf16[256,256]{1,0:T(8,128)(2,1)} %constant.25.clone.waves_ref) | copy-start | bytes 393220
  11.9 0.8 copy-start.13
  12.7 0.7 copy-start.14
  13.3 0.7 copy-start.15
  14.0 0.7 copy-start.16
  14.6 0.7 copy-start.17
  15.3 0.7 copy-start.18
  16.0 61.8 %copy-start.1 = (f32[2,32,32,256]{3,2,1,0:T(8,128)S(1)}, f32[2,32,32,256]{3,2,1,0:T(8,128)}, u32[]{:S(2)}) copy-start(f32[2,32,32,256]{3,2,1,0:T(8,128)} %mod.1) | copy-start | bytes 6291460
  16.0 61.8 %copy-start.3 = (bf16[3,128,224]{2,1,0:T(8,128)(2,1)S(1)}, bf16[3,128,224]{2,1,0:T(8,128)(2,1)}, u32[]{:S(2)}) copy-start(bf16[3,128,224]{2,1,0:T(8,128)(2,1)} %constant.20.clone.cross_ref) | copy-start | bytes 516100
where the time goes:
time: 88.1 us; the launch traced here: 87.4 us
  Pallas kernels  71.4 us (81%)
  local copies, waits for them, and re-layouts  14.7 us (17%)
  between operations  1.33 us (2%)
    pallas_call x1, Pallas kernels, shards(): pl.pallas_call(main_kernel, out_shape=[block, block, jax.ShapeDtypeStruct...  61.8 us
    unnamed x38, local copies, waits for them, and re-layouts  14.7 us
    pallas_call x1, Pallas kernels, shards(): pl.pallas_call(last_kernel, grid=(GROUPS,), out_shape=[block, block], in_...  9.66 us

commit v1 on v0

v1 whole, which is shorter than its diff:
```python
import functools
import math

import jax
import jax.numpy as jnp
import ml_dtypes
import numpy as np
from jax import lax
from jax.experimental import pallas as pl
from jax.experimental.pallas import tpu as pltpu
from jax.sharding import PartitionSpec as P

F = 128
NK = 1024
NR = 2048
ND = 32
STEPS = 4
TSTART = 32
GX = 16
GY = 8
C = 32
NZ = 256
Q = 256
GROUPS = 8
XG = 4
ROWS = XG * C
LINKS = 12
VMEM = 63 * 1024 * 1024
MESH = pl.DeviceIdType.MESH
BF = jnp.bfloat16
F32 = jnp.float32


def constants():
    y2 = np.zeros((ROWS, ROWS + 32), np.float32)
    y1 = np.zeros((ROWS, ROWS + 32), np.float32)
    low, high = ROWS, ROWS + 16

    def place(x, y):
        if y < 0:
            return low + 2 * (x + 1) + y + 2
        if y >= C:
            return high + 2 * (x + 1) + y - C
        return x * C + y

    for x in range(XG):
        for y in range(C):
            row = x * C + y
            for shift, factor in ((-2, -1.0), (-1, 16.0), (1, 16.0), (2, -1.0)):
                y2[row, place(x, y + shift)] += factor
            y1[row, place(x, y + 1)] += 1.0
            y1[row, place(x, y - 1)] -= 1.0
    cross = np.zeros((3, ROWS, ROWS + 96), np.float32)
    for kind in range(3):
        cross[kind, :, :ROWS] = 3.0 * y1[:, :ROWS]
        cross[kind, :, ROWS + 64 :] = 3.0 * y1[:, ROWS:]
        for x in range(XG):
            for y, beyond, sign in ((0, -1, -3.0), (C - 1, C, 3.0)):
                for step in (-1, 1):
                    outside = (kind == 0 and x + step < 0) or (kind == 2 and x + step >= XG)
                    if outside:
                        spot = ROWS + 32 + 15 if beyond < 0 else ROWS + 48
                    else:
                        spot = place(x + step, beyond)
                    cross[kind, x * C + y, spot] += sign * step
    pick = np.zeros((3, 32, 6 * C), np.float32)
    for kind in range(3):
        for i in range(6):
            x = i - 1 + kind
            if 0 <= x < 6:
                for k in range(2):
                    pick[kind, 2 * i + k, x * C + C - 2 + k] = 1.0
                    pick[kind, 16 + 2 * i + k, x * C + k] = 1.0
    z2 = np.zeros((NZ, NZ), np.float32)
    z1 = np.zeros((NZ, NZ), np.float32)
    for z in range(NZ):
        for shift, factor in ((-2, -1.0), (-1, 16.0), (1, 16.0), (2, -1.0)):
            if 0 <= z + shift < NZ:
                z2[z + shift, z] += factor
        if z + 1 < NZ:
            z1[z + 1, z] += 1.0
        if z > 0:
            z1[z - 1, z] -= 1.0
    period = 2 * F
    turns = (np.arange(F)[None, :] + 1) * (TSTART + np.arange(STEPS)[:, None]) % period
    angles = turns * (2.0 * math.pi / period)
    weight = 1.0 / math.sqrt(F)
    waves = np.concatenate([weight * np.cos(angles), -weight * np.sin(angles)], axis=1).T
    waves = np.repeat(waves.astype(np.float32), ND, axis=1)
    upper = waves.astype(ml_dtypes.bfloat16)
    lower = (waves - upper.astype(np.float32)).astype(ml_dtypes.bfloat16)
    half = ml_dtypes.bfloat16
    parts = [y2, y1, *cross, z2, z1, 3.0 * z1, *pick]
    parts = [np.pad(part, ((0, 0), (0, 256 - part.shape[1]))).astype(half) for part in parts]
    return np.concatenate(parts + [np.concatenate([upper, lower], axis=1)])


AT_Y2, AT_Y1, AT_CROSS, AT_Z2, AT_Z1, AT_Z3 = 0, 128, 256, 640, 896, 1152
AT_PICK, AT_WAVES, TABLE = 1408, 1504, 1760
SHORT = AT_PICK


def matrices(table, kind):
    return (
        table[AT_Y2 : AT_Y2 + ROWS, : ROWS + 32],
        table[AT_Y1 : AT_Y1 + ROWS, : ROWS + 32],
        table[pl.ds(pl.multiple_of(AT_CROSS + ROWS * kind, ROWS), ROWS)],
        table[AT_Z2 : AT_Z2 + NZ],
        table[AT_Z1 : AT_Z1 + NZ],
        table[AT_Z3 : AT_Z3 + NZ],
    )


def dot(a, b):
    return jnp.dot(a, b, preferred_element_type=F32)


def beside(*parts):
    return jnp.concatenate(parts, axis=1)


def below(*parts):
    return jnp.concatenate(parts, axis=0)


def advance(window, lows, highs, clows, chighs, now, before, lam, mu, sources, y2, y1, cross, z2, z1, z3):
    wide = [w.astype(F32) for w in window]
    inner = [w[2 : 2 + XG].reshape(ROWS, NZ) for w in window]
    second = [(16.0 * (w[1:5] + w[3:7]) - (w[0:4] + w[4:8])).reshape(ROWS, NZ) for w in wide]
    first = [(w[3:7] - w[1:5]).reshape(ROWS, NZ) for w in wide]
    tall = [below(inner[c], lows[c], highs[c]) for c in range(3)]
    skew_z = dot(tall[2], z1)
    skew_y = dot(y1, tall[1])
    lap = [dot(beside(inner[c], y2), below(z2, tall[c])) for c in range(3)]
    mix_0 = dot(
        beside(first[2].astype(BF), cross[:, : ROWS + 64]),
        below(z3, first[1].astype(BF), lows[1], highs[1], clows[1], chighs[1]),
    )
    mix_1 = dot(
        beside(cross, y2),
        below(
            (first[0] + skew_z[:ROWS]).astype(BF), lows[0], highs[0], clows[0], chighs[0],
            skew_z[ROWS:].astype(BF), lows[0], highs[0], tall[1],
        ),
    )
    mix_2 = dot(beside(inner[2], (first[0] + skew_y).astype(BF)), below(z2, z3))
    couple = [second[0] + mix_0, mix_1, mix_2]
    shear = mu * (1.0 / 12.0)
    joint = (lam + mu) * (1.0 / 12.0)
    centre = 2.0 - 90.0 * shear - 30.0 * joint
    result = []
    for c in range(3):
        moved = shear * (second[c] + lap[c]) + joint * couple[c]
        if sources is not None:
            moved = moved + sources[c]
        result.append((centre * now[c] - before[c]) + moved)
    return result


def sine(x):
    y = x * x
    poly = -2.5052108e-08
    for coefficient in (2.7557319e-06, -1.9841270e-04, 8.3333333e-03, -1.6666667e-01, 1.0):
        poly = poly * y + coefficient
    return x * poly


def cosine(x):
    y = x * x
    poly = -2.7557319e-07
    for coefficient in (2.4801587e-05, -1.3888889e-03, 4.1666667e-02, -0.5, 1.0):
        poly = poly * y + coefficient
    return poly


def lane_spread(row):
    return jnp.transpose(jnp.broadcast_to(row.astype(F32), (128, 128))).astype(jnp.int32)


def main_kernel(
    slow_ref, rigid_ref, damp_ref, level_ref, live_ref, target_ref,
    table_hbm, offsets_hbm, levels_hbm, moduli_hbm, old_hbm, now_hbm,
    last_hbm, prior_hbm, half_hbm, side_hbm, corner_hbm, spread_hbm,
    field, mod, half, side_out, side_in, corner, hot, gathered, basis, spread,
    table, slot_tile, zbuf, ebuf, dbuf, kbuf,
    load_sem, store_sem, group_sem, send_sem, recv_sem, gsend_sem, grecv_sem,
):
    gx = lax.axis_index("gx")
    gy = lax.axis_index("gy")
    device = gx * GY + gy
    px, pz = gx // 4, gx % 4
    py, core = gy // 2, gy % 2
    block = core * 64 + px * 16 + pz * 4 + py

    loads = [
        pltpu.make_async_copy(now_hbm, field.at[0], load_sem.at[0]),
        pltpu.make_async_copy(old_hbm, field.at[1], load_sem.at[1]),
        pltpu.make_async_copy(moduli_hbm, mod, load_sem.at[2]),
        pltpu.make_async_copy(
            offsets_hbm.at[pl.ds(pl.multiple_of(device // 4 * 8, 8), 8)], slot_tile.at[0], load_sem.at[3]
        ),
        pltpu.make_async_copy(
            levels_hbm.at[pl.ds(pl.multiple_of(device // 4 * 8, 8), 8)], slot_tile.at[1], load_sem.at[4]
        ),
        pltpu.make_async_copy(table_hbm, table, load_sem.at[5]),
    ]
    for load in loads:
        load.start()

    for p in range(2):
        half[p, :, 0:2] = jnp.zeros((3, 2, C, NZ), BF)
        half[p, :, C + 2 : C + 4] = jnp.zeros((3, 2, C, NZ), BF)
        corner[p] = jnp.zeros(corner.shape[1:], BF)
        for s in range(2):
            side_in[p, s] = jnp.zeros(side_in.shape[2:], BF)

    steps = [(1, 0), (-1, 0), (0, 1), (0, -1), (1, 1), (1, -1), (-1, 1), (-1, -1)]

    def exists(dx, dy):
        ok = None
        for delta, place, size in ((dx, gx, GX), (dy, gy, GY)):
            if delta == 1:
                part = place < size - 1
            elif delta == -1:
                part = place > 0
            else:
                continue
            ok = part if ok is None else jnp.logical_and(ok, part)
        return ok

    barrier = pltpu.get_barrier_semaphore()
    for dx, dy in steps:
        @pl.when(exists(dx, dy))
        def _():
            pl.semaphore_signal(barrier, inc=1, device_id=(gx + dx, gy + dy), device_id_type=MESH)

    def ring_y(k):
        return (gx, (py + k) % 4 * 2 + core)

    def ring_z(k):
        return (px * 4 + (pz + k) % 4, gy)

    def ring_x(k):
        return ((px + k) % 4 * 4 + pz, gy)

    for ring in (ring_y, ring_z, ring_x):
        for k in (1, 2, 3):
            pl.semaphore_signal(barrier, inc=1, device_id=ring(k), device_id_type=MESH)
    twin = (gx, py * 2 + 1 - core)
    pl.semaphore_signal(barrier, inc=1, device_id=twin, device_id_type=MESH)

    rows = lax.broadcasted_iota(jnp.int32, (8, 128), 0) + block * 8
    wavenum = (rows.astype(F32) + 0.5) * (4.0 / NK)
    square_k = wavenum * wavenum
    omega = (lax.broadcasted_iota(jnp.int32, (8, 128), 1) + 1).astype(F32) * (4.0 / F)

    def downward(i, carry):
        down_re, down_im = carry
        layer = level_ref[i]
        part = omega * slow_ref[layer]
        vertical = jnp.sqrt(square_k + part * part)
        fade = jnp.exp(vertical * (-0.25 * damp_ref[layer]))
        angle = 0.125 * vertical
        s, c = sine(angle), cosine(angle)
        leg_re = fade * (1.0 - 2.0 * s * s)
        leg_im = fade * (-2.0 * s * c)
        zbuf[i] = rigid_ref[layer] * vertical
        ebuf[0, i] = leg_re
        ebuf[1, i] = leg_im
        dbuf[0, i] = down_re
        dbuf[1, i] = down_im
        return down_re * leg_re - down_im * leg_im, down_re * leg_im + down_im * leg_re

    one = jnp.ones((8, 128), F32)
    zero = jnp.zeros((8, 128), F32)
    lax.fori_loop(0, ND, downward, (one, zero), unroll=4)
    zbuf[ND] = zbuf[ND - 1]

    def upward(step, carry):
        refl_re, refl_im = carry
        i = ND - 1 - step
        upper, under = zbuf[i], zbuf[i + 1]
        r = (upper - under) / (upper + under)
        leg_re, leg_im = ebuf[0, i], ebuf[1, i]
        trip_re = leg_re * leg_re - leg_im * leg_im
        trip_im = 2.0 * leg_re * leg_im
        upper_re = r + refl_re
        lower_re = 1.0 + r * refl_re
        lower_im = r * refl_im
        scale = 1.0 / (lower_re * lower_re + lower_im * lower_im)
        ratio_re = (upper_re * lower_re + refl_im * lower_im) * scale
        ratio_im = (refl_im * lower_re - upper_re * lower_im) * scale
        fresh_re = trip_re * ratio_re - trip_im * ratio_im
        fresh_im = trip_re * ratio_im + trip_im * ratio_re
        down_re, down_im = dbuf[0, i], dbuf[1, i]
        kbuf[i, :, 0:128] = (down_re * (1.0 + fresh_re) - down_im * fresh_im) * (1.0 / 32.0)
        kbuf[i, :, 128:256] = (down_re * fresh_im + down_im * (1.0 + fresh_re)) * (1.0 / 32.0)
        return fresh_re, fresh_im

    lax.fori_loop(0, ND, upward, (zero, zero), unroll=4)
    loads[5].wait()
    product = dot(kbuf[...].reshape(ND * 8, 2 * F).astype(BF), table[AT_WAVES : AT_WAVES + 2 * F])
    product = product[:, :128] + product[:, 128:]
    lane = lax.broadcasted_iota(jnp.int32, (8, 128), 1) % ND
    mine = zero
    for d in range(ND):
        mine = jnp.where(lane == d, product[8 * d : 8 * d + 8], mine)
    gathered[block] = mine

    count = 10
    for dx, dy in steps:
        count = count + exists(dx, dy).astype(jnp.int32)
    pl.semaphore_wait(barrier, count)

    def stage(index, ring, start, size):
        copies = []
        for k in (1, 2, 3):
            piece = gathered.at[pl.ds(start, size)]
            copies.append(
                pltpu.make_async_remote_copy(
                    src_ref=piece,
                    dst_ref=piece,
                    send_sem=gsend_sem.at[3 * index + k - 1],
                    recv_sem=grecv_sem.at[3 * index + k - 1],
                    device_id=ring(k),
                    device_id_type=MESH,
                )
            )
        for copy in copies:
            copy.start()
        return copies

    def finish(copies):
        for copy in copies:
            copy.wait()

    stage_y = stage(0, ring_y, block, 1)

    batches = [(6, 2), (0, 3), (3, 3)]

    def message(n, index):
        p = n % 2
        if index < 2:
            move = (1, 0) if index == 0 else (-1, 0)
            source = half.at[p, :, pl.ds(C if index == 0 else 2, 2)]
            target = half.at[p, :, pl.ds(0 if index == 0 else C + 2, 2)]
        elif index < 6:
            move = (1 if index < 4 else -1, 1 if index % 2 == 0 else -1)
            source = half.at[
                p, pl.ds(0, 2), C + 1 if move[0] == 1 else 2, pl.ds(16 if move[1] == 1 else 0, 16)
            ]
            target = corner.at[p, 0 if move[0] == 1 else 2, 0 if move[1] == 1 else 1]
        else:
            s, (first, size) = (index - 6) // 3, batches[(index - 6) % 3]
            move = (0, 1) if s == 0 else (0, -1)
            source = side_out.at[p, s, pl.ds(first, size)]
            target = side_in.at[p, s, pl.ds(first, size)]
        copy = pltpu.make_async_remote_copy(
            src_ref=source,
            dst_ref=target,
            send_sem=send_sem.at[n, index],
            recv_sem=recv_sem.at[n, index],
            device_id=(gx + move[0], gy + move[1]),
            device_id_type=MESH,
        )
        return copy, exists(*move), exists(-move[0], -move[1])

    def start(n, *indices):
        for index in indices:
            copy, there, _ = message(n, index)

            @pl.when(there)
            def _():
                copy.start()

    def arrive(n, *indices):
        for index in indices:
            copy, _, here = message(n, index)

            @pl.when(here)
            def _():
                copy.wait_recv()

    def sent(n):
        for index in range(LINKS):
            copy, there, _ = message(n, index)

            @pl.when(there)
            def _():
                copy.wait_send()

    def kind_of(g):
        return jnp.where(g == 0, 0, jnp.where(g == GROUPS - 1, 2, 1))

    def fill(n, first, size):
        p = n % 2

        def one_tile(g, carry):
            kind = kind_of(g)
            x = jnp.where(g == 0, 0, jnp.where(g == GROUPS - 1, C - 6, g * XG - 1))
            pick = table[pl.ds(pl.multiple_of(AT_PICK + 32 * kind, 32), 32), : 6 * C]
            for c in range(3):
                tile = dot(pick, half[p, c, pl.ds(x + 2, 6)].reshape(6 * C, NZ)).astype(BF)
                side_out[p, 0, g, c] = tile[:16]
                side_out[p, 1, g, c] = tile[16:]
            return carry

        lax.fori_loop(first, first + size, one_tile, 0)

    def group_at(i):
        return jnp.where(i < 3, GROUPS - 1 - i, i - 3)

    def publish(n, i):
        @pl.when(i == 0)
        def _():
            start(n, 0, 2, 3)

        @pl.when(i == 2)
        def _():
            fill(n, *batches[0])
            start(n, 6, 9)

        @pl.when(i == 3)
        def _():
            start(n, 1, 4, 5)

        @pl.when(i == 6)
        def _():
            fill(n, *batches[1])
            start(n, 7, 10)

        @pl.when(i == 7)
        def _():
            fill(n, *batches[2])
            start(n, 8, 11)

    def receive(n, i):
        @pl.when(i == 0)
        def _():
            arrive(n, 1, 4, 5, 6, 9)

        @pl.when(i == 2)
        def _():
            arrive(n, 8, 11)

        @pl.when(i == 3)
        def _():
            arrive(n, 0, 2, 3, 7, 10)

    def update(n, g, sources):
        p = n % 2
        x = g * XG
        kind = kind_of(g)
        return advance(
            [half[p, c, pl.ds(x, XG + 4)] for c in range(3)],
            [side_in[p, 0, g, c] for c in range(3)],
            [side_in[p, 1, g, c] for c in range(3)],
            [corner[p, kind, 0, c] for c in range(2)],
            [corner[p, kind, 1, c] for c in range(2)],
            [field[p, c, pl.ds(x, XG)].reshape(ROWS, NZ) for c in range(3)],
            [field[1 - p, c, pl.ds(x, XG)].reshape(ROWS, NZ) for c in range(3)],
            mod[0, pl.ds(x, XG)].reshape(ROWS, NZ),
            mod[1, pl.ds(x, XG)].reshape(ROWS, NZ),
            sources,
            *matrices(table, kind),
        )

    def injected(n, g):
        values = dot(hot[g].reshape(3 * ROWS, Q), spread[n])
        return [values[ROWS * c : ROWS * c + ROWS] for c in range(3)]

    def keep(n, g, c, fresh):
        x = g * XG
        fresh = fresh.reshape(XG, C, NZ)
        field[n % 2, c, pl.ds(x, XG)] = fresh
        half[n % 2, c, pl.ds(x + 2, XG)] = fresh.astype(BF)

    def to_half(g, carry):
        x = g * XG
        for c in range(3):
            half[0, c, pl.ds(x + 2, XG)] = field[0, c, pl.ds(x, XG)].astype(BF)
        return carry

    loads[0].wait()
    lax.fori_loop(0, GROUPS, to_half, 0)
    start(0, 0, 1, 2, 3, 4, 5)
    fill(0, 0, GROUPS)
    start(0, 6, 7, 8, 9, 10, 11)
    finish(stage_y)
    stage_z = stage(1, ring_z, block // 4 * 4, 4)

    loads[3].wait()
    loads[4].wait()
    row = device % 4 * 2
    mask = NK * NR // 2 - 1
    for h in range(2):
        part = pl.ds(128 * h, 128)
        q = lane_spread(slot_tile[0, pl.ds(row + h, 1)])
        lanes = lax.broadcasted_iota(jnp.int32, (128, 128), 1)
        for b in range(NK // 128):
            turns = (2 * (lanes + 128 * b) + 1) * q
            turns = ((turns + (mask + 1) // 2) & mask) - (mask + 1) // 2
            s = sine(turns.astype(F32) * (math.pi / (mask + 1)))
            basis[part, 128 * b : 128 * b + 128] = (1.0 - 2.0 * s * s).astype(BF)
    finish(stage_z)
    stage_x = stage(2, ring_x, block // 16 * 16, 16)

    def build_hot(g, carry):
        ids = lax.broadcasted_iota(jnp.int32, (ROWS, Q), 0) + g * ROWS
        columns = target_ref[...] // NZ
        for c in range(3):
            same = ids + c * C * C == columns
            hot[g, c] = jnp.where(same, 1.0, 0.0).astype(BF)
        return carry

    lax.fori_loop(0, GROUPS, build_hot, 0)
    loads[1].wait()
    loads[2].wait()
    whole = gathered.at[pl.ds(core * 64, 64)]
    swap = pltpu.make_async_remote_copy(
        src_ref=whole,
        dst_ref=whole,
        send_sem=gsend_sem.at[9],
        recv_sem=grecv_sem.at[9],
        device_id=twin,
        device_id_type=MESH,
    )

    def first_step(i, carry):
        receive(0, i)

        @pl.when(i == 4)
        def _():
            finish(stage_x)
            swap.start()

        g = group_at(i)
        result = update(0, g, None)
        for c in range(3):
            field[1, c, pl.ds(g * XG, XG)] = result[c].reshape(XG, C, NZ)
        return carry

    lax.fori_loop(0, GROUPS, first_step, 0)
    swap.wait()

    total = gathered[...].reshape(NK, 128)
    upper = total.astype(BF)
    lower = (total - upper.astype(F32)).astype(BF)
    picked = dot(basis[...], jnp.concatenate([upper, lower], axis=1))
    picked = picked[:, :128] + picked[:, 128:]
    ones = jnp.ones((128, NZ), BF)
    for h in range(2):
        part = slice(128 * h, 128 * h + 128)
        lanes = lax.broadcasted_iota(jnp.int32, (128, 128), 1)
        ids = lax.broadcasted_iota(jnp.int32, (128, 128), 0) + 128 * h
        level = lane_spread(slot_tile[1, pl.ds(row + h, 1)])
        live = jnp.logical_and(lanes % ND == level, ids < live_ref[0])
        chosen = jnp.where(live, picked[part], 0.0)
        depth = lane_spread(target_ref[:, 128 * h : 128 * h + 128] % NZ)
        for n in range(STEPS):
            values = dot(jnp.where(lanes // ND == n, chosen, 0.0).astype(BF), ones)
            for b in range(2):
                same = lanes + 128 * b == depth
                spread[n, part, 128 * b : 128 * b + 128] = jnp.where(
                    same, values[:, 128 * b : 128 * b + 128], 0.0
                ).astype(BF)

    def first_sources(i, carry):
        g = group_at(i)
        sources = injected(0, g)
        for c in range(3):
            keep(1, g, c, field[1, c, pl.ds(g * XG, XG)].reshape(ROWS, NZ) + sources[c])
        publish(1, i)
        return carry

    lax.fori_loop(0, GROUPS, first_sources, 0)

    spread_store = pltpu.make_async_copy(spread.at[STEPS - 1], spread_hbm, store_sem.at[0])
    spread_store.start()
    prior_store = pltpu.make_async_copy(field.at[0], prior_hbm, store_sem.at[1])

    def last_stores(g):
        x = g * XG
        return (
            pltpu.make_async_copy(
                field.at[1, :, pl.ds(x, XG)], last_hbm.at[:, pl.ds(x, XG)], group_sem.at[0, g]
            ),
            pltpu.make_async_copy(
                half.at[1, :, pl.ds(x + 2, XG)], half_hbm.at[:, pl.ds(x + 2, XG)], group_sem.at[1, g]
            ),
        )

    for n in range(1, STEPS - 1):
        sent(n - 1)
        if n == STEPS - 2:
            prior_store.start()

        def later_step(i, carry):
            receive(n, i)
            g = group_at(i)
            result = update(n, g, injected(n, g))
            for c in range(3):
                keep(n + 1, g, c, result[c])
            publish(n + 1, i)
            if n == STEPS - 2:
                for store in last_stores(g):
                    store.start()
            return carry

        lax.fori_loop(0, GROUPS, later_step, 0)

    last = STEPS - 1
    arrive(last, 0, 1)
    ends = [
        pltpu.make_async_copy(half.at[1, :, pl.ds(x, 2)], half_hbm.at[:, pl.ds(x, 2)], store_sem.at[k])
        for x, k in ((0, 2), (C + 2, 3))
    ]
    for store in ends:
        store.start()
    arrive(last, 2, 3, 4, 5)
    corner_store = pltpu.make_async_copy(corner.at[1], corner_hbm, store_sem.at[4])
    corner_store.start()
    arrive(last, 6, 7, 8, 9, 10, 11)
    side_store = pltpu.make_async_copy(side_in.at[1], side_hbm, store_sem.at[5])
    side_store.start()
    sent(last - 1)
    sent(last)
    for store in (spread_store, prior_store, *ends, corner_store, side_store):
        store.wait()

    def drain(g, carry):
        for store in last_stores(g):
            store.wait()
        return carry

    lax.fori_loop(0, GROUPS, drain, 0)


def last_kernel(
    target_ref,
    table_hbm, half_hbm, side_hbm, corner_hbm, spread_hbm, now_hbm, before_hbm, moduli_hbm,
    final_hbm, copy_hbm,
    table, half, side, corner, spread, now, before, mod, final,
    sem, half_sem, load_sem, store_sem,
):
    small = [
        pltpu.make_async_copy(source, target, sem.at[k])
        for k, (source, target) in enumerate(
            (
                (table_hbm.at[pl.ds(0, SHORT)], table),
                (spread_hbm, spread),
                (side_hbm, side),
                (corner_hbm, corner),
            )
        )
    ]

    def half_load(k):
        x = k * XG
        return pltpu.make_async_copy(half_hbm.at[:, pl.ds(x, XG)], half.at[:, pl.ds(x, XG)], half_sem.at[k])

    def group_loads(g):
        part = pl.ds(g * XG, XG)
        return [
            pltpu.make_async_copy(source.at[:, part], target.at[:, part], load_sem.at[k, g])
            for k, (source, target) in enumerate(
                ((now_hbm, now), (before_hbm, before), (moduli_hbm, mod))
            )
        ]

    def group_stores(g):
        part = pl.ds(g * XG, XG)
        return [
            pltpu.make_async_copy(source.at[:, part], target.at[:, part], store_sem.at[k, g])
            for k, (source, target) in enumerate(((final, final_hbm), (now, copy_hbm)))
        ]

    half_load(0).start()
    for load in small:
        load.start()

    def begin(g, carry):
        half_load(g + 1).start()
        for load in group_loads(g):
            load.start()
        return carry

    lax.fori_loop(0, GROUPS, begin, 0)
    half_load(0).wait()
    for load in small:
        load.wait()

    def group(g, carry):
        x = g * XG
        half_load(g + 1).wait()
        for load in group_loads(g):
            load.wait()
        stores = group_stores(g)
        stores[1].start()
        kind = jnp.where(g == 0, 0, jnp.where(g == GROUPS - 1, 2, 1))
        ids = lax.broadcasted_iota(jnp.int32, (ROWS, Q), 0) + g * ROWS
        columns = target_ref[...] // NZ
        hot = [jnp.where(ids + c * C * C == columns, 1.0, 0.0).astype(BF) for c in range(3)]
        values = dot(below(*hot), spread[...])
        result = advance(
            [half[c, pl.ds(x, XG + 4)] for c in range(3)],
            [side[0, g, c] for c in range(3)],
            [side[1, g, c] for c in range(3)],
            [corner[kind, 0, c] for c in range(2)],
            [corner[kind, 1, c] for c in range(2)],
            [now[c, pl.ds(x, XG)].reshape(ROWS, NZ) for c in range(3)],
            [before[c, pl.ds(x, XG)].reshape(ROWS, NZ) for c in range(3)],
            mod[0, pl.ds(x, XG)].reshape(ROWS, NZ),
            mod[1, pl.ds(x, XG)].reshape(ROWS, NZ),
            [values[ROWS * c : ROWS * c + ROWS] for c in range(3)],
            *matrices(table, kind),
        )
        for c in range(3):
            final[c, pl.ds(x, XG)] = result[c].reshape(XG, C, NZ)
        stores[0].start()
        return carry

    lax.fori_loop(0, GROUPS, group, 0)

    def drain(g, carry):
        for store in group_stores(g):
            store.wait()
        return carry

    lax.fori_loop(0, GROUPS, drain, 0)


def shards(
    layer_slowness, layer_rigidity, layer_damping, layer_of_level,
    slot_offset, slot_level, slot_target, live_count, moduli, field_old, field_now,
):
    fixed = jnp.asarray(constants())
    smem = pl.BlockSpec(memory_space=pltpu.SMEM)
    vmem = pl.BlockSpec(memory_space=pltpu.VMEM)
    any_space = pl.BlockSpec(memory_space=pl.ANY)
    target = slot_target.reshape(1, Q)
    block = jax.ShapeDtypeStruct((3, C, C, NZ), F32)
    dma = pltpu.SemaphoreType.DMA
    last, prior, half, side, corner, spread = pl.pallas_call(
        main_kernel,
        out_shape=[
            block,
            block,
            jax.ShapeDtypeStruct((3, C + 4, C, NZ), BF),
            jax.ShapeDtypeStruct((2, GROUPS, 3, 16, NZ), BF),
            jax.ShapeDtypeStruct((3, 2, 2, 16, NZ), BF),
            jax.ShapeDtypeStruct((Q, NZ), BF),
        ],
        in_specs=[smem] * 5 + [vmem] + [any_space] * 6,
        out_specs=[any_space] * 6,
        scratch_shapes=[
            pltpu.VMEM((2, 3, C, C, NZ), F32),
            pltpu.VMEM((2, C, C, NZ), F32),
            pltpu.VMEM((2, 3, C + 4, C, NZ), BF),
            pltpu.VMEM((2, 2, GROUPS, 3, 16, NZ), BF),
            pltpu.VMEM((2, 2, GROUPS, 3, 16, NZ), BF),
            pltpu.VMEM((2, 3, 2, 2, 16, NZ), BF),
            pltpu.VMEM((GROUPS, 3, ROWS, Q), BF),
            pltpu.VMEM((NK // 8, 8, 128), F32),
            pltpu.VMEM((Q, NK), BF),
            pltpu.VMEM((STEPS, Q, NZ), BF),
            pltpu.VMEM((TABLE, NZ), BF),
            pltpu.VMEM((2, 8, 128), jnp.int32),
            pltpu.VMEM((ND + 1, 8, 128), F32),
            pltpu.VMEM((2, ND, 8, 128), F32),
            pltpu.VMEM((2, ND, 8, 128), F32),
            pltpu.VMEM((ND, 8, 2 * F), F32),
            dma((6,)),
            dma((6,)),
            dma((2, GROUPS)),
            dma((STEPS, LINKS)),
            dma((STEPS, LINKS)),
            dma((10,)),
            dma((10,)),
        ],
        compiler_params=pltpu.CompilerParams(
            collective_id=0, has_side_effects=True, vmem_limit_bytes=VMEM
        ),
    )(
        layer_slowness, layer_rigidity, layer_damping, layer_of_level, live_count, target,
        fixed,
        slot_offset.reshape(Q, 128), slot_level.reshape(Q, 128), moduli, field_old, field_now,
    )

    return pl.pallas_call(
        last_kernel,
        out_shape=[block, block],
        in_specs=[vmem] + [any_space] * 8,
        out_specs=[any_space] * 2,
        scratch_shapes=[
            pltpu.VMEM((SHORT, NZ), BF),
            pltpu.VMEM(half.shape, BF),
            pltpu.VMEM(side.shape, BF),
            pltpu.VMEM(corner.shape, BF),
            pltpu.VMEM(spread.shape, BF),
            pltpu.VMEM((3, C, C, NZ), F32),
            pltpu.VMEM((3, C, C, NZ), F32),
            pltpu.VMEM((2, C, C, NZ), F32),
            pltpu.VMEM((3, C, C, NZ), F32),
            dma((4,)),
            dma((GROUPS + 1,)),
            dma((3, GROUPS)),
            dma((2, GROUPS)),
        ],
        compiler_params=pltpu.CompilerParams(vmem_limit_bytes=VMEM),
    )(target, fixed, half, side, corner, spread, last, prior, moduli)


def solution(mesh):
    in_specs = (
        P(),
        P(),
        P(),
        P(),
        P(),
        P(),
        P(("gx", "gy")),
        P(("gx", "gy")),
        P(None, "gx", "gy", None),
        P(None, "gx", "gy", None),
        P(None, "gx", "gy", None),
    )
    out_specs = (P(None, "gx", "gy", None), P(None, "gx", "gy", None))
    return jax.shard_map(shards, mesh=mesh, in_specs=in_specs, out_specs=out_specs, check_vma=False)
```

time: 88.1 us -> 58.9 us (0.67)
  the two profiles are of different devices: /device:TPU:3 before, /device:TPU:1 now
where the time goes in v1:
time: 58.9 us; the launch traced here: 58.8 us
  Pallas kernels  57.5 us (98%)
  between operations  1.29 us (2%)
    pallas_call x1, Pallas kernels, shards(): pl.pallas_call(main_kernel, out_shape=[block, block, jax.ShapeDtypeStruct...  49.2 us
    pallas_call x1, Pallas kernels, shards(): pl.pallas_call(last_kernel, out_shape=[block, block], in_specs=[vmem] + [...  8.25 us

profile of v1, /device:TPU:1, one launch (start us, length us, event | category | flops | bytes accessed | tf_op | source)
XLA Modules:
  0.0 58.8 jit_solution(9340554769154842091)
XLA Ops:
  1.3 49.2 %shard_map.131 = (f32[3,32,32,256]{3,2,1,0:T(8,128)}, f32[3,32,32,256]{3,2,1,0:T(8,128)}, bf16[3,36,32,256]{3,2,1,0:T(8,128)(2,1)}, bf16[2,8,3,16,256]{4,3,2,1,0...) custom-call(f32[8]{0:T(128)} %slow_ref.1, f32[8]{0:T(128)} %rigid_ref.1, f32[8]{0:T(128)} %damp_ref.1, ...), custom_call_target="tpu_custom_call" | custom-call | tf_op jit(solution)/shard_map/pallas_call | solution.py:744
  50.5 8.2 %shard_map.132 = (f32[3,32,32,256]{3,2,1,0:T(8,128)}, f32[3,32,32,256]{3,2,1,0:T(8,128)}) custom-call(s32[1,256]{1,0:T(1,128)} %bitcast.6, bf16[1760,256]{1,0:T(8,128)(2,1)} %constant.2.clone.table_hbm, bf16[3,36,32,256]{3,2,1,0:T(8,128)(2,1)} %get-tuple-element.8.half_hbm, bf16[2,8,3,16,256]{4,3,2,1,0:T(8,128)(2,1)} %get-tuple-element.9.side_hbm, ...), custom_call_target="tpu_custom_call" | custom-call | tf_op jit(solution)/shard_map/pallas_call | solution.py:790

commit v2 on v1

--- a/solution.py
+++ b/solution.py
@@ -32,28 +32,28 @@
 
 
 def constants():
-    y2 = np.zeros((ROWS, ROWS + 32), np.float32)
-    y1 = np.zeros((ROWS, ROWS + 32), np.float32)
     low, high = ROWS, ROWS + 16
 
-    def place(x, y):
+    def place(x, y, kind):
         if y < 0:
-            return low + 2 * (x + 1) + y + 2
+            return low + 8 * (y + 2) + x + (0, 1, 4)[kind]
         if y >= C:
-            return high + 2 * (x + 1) + y - C
+            return high + 8 * (y - C) + x + (0, 1, 4)[kind]
         return x * C + y
 
-    for x in range(XG):
-        for y in range(C):
-            row = x * C + y
-            for shift, factor in ((-2, -1.0), (-1, 16.0), (1, 16.0), (2, -1.0)):
-                y2[row, place(x, y + shift)] += factor
-            y1[row, place(x, y + 1)] += 1.0
-            y1[row, place(x, y - 1)] -= 1.0
+    y2 = np.zeros((3, ROWS, ROWS + 32), np.float32)
+    y1 = np.zeros((3, ROWS, ROWS + 32), np.float32)
     cross = np.zeros((3, ROWS, ROWS + 96), np.float32)
     for kind in range(3):
-        cross[kind, :, :ROWS] = 3.0 * y1[:, :ROWS]
-        cross[kind, :, ROWS + 64 :] = 3.0 * y1[:, ROWS:]
+        for x in range(XG):
+            for y in range(C):
+                row = x * C + y
+                for shift, factor in ((-2, -1.0), (-1, 16.0), (1, 16.0), (2, -1.0)):
+                    y2[kind, row, place(x, y + shift, kind)] += factor
+                y1[kind, row, place(x, y + 1, kind)] += 1.0
+                y1[kind, row, place(x, y - 1, kind)] -= 1.0
+        cross[kind, :, :ROWS] = 3.0 * y1[kind, :, :ROWS]
+        cross[kind, :, ROWS + 64 :] = 3.0 * y1[kind, :, ROWS:]
         for x in range(XG):
             for y, beyond, sign in ((0, -1, -3.0), (C - 1, C, 3.0)):
                 for step in (-1, 1):
@@ -61,16 +61,8 @@
                     if outside:
                         spot = ROWS + 32 + 15 if beyond < 0 else ROWS + 48
                     else:
-                        spot = place(x + step, beyond)
+                        spot = place(x + step, beyond, kind)
                     cross[kind, x * C + y, spot] += sign * step
-    pick = np.zeros((3, 32, 6 * C), np.float32)
-    for kind in range(3):
-        for i in range(6):
-            x = i - 1 + kind
-            if 0 <= x < 6:
-                for k in range(2):
-                    pick[kind, 2 * i + k, x * C + C - 2 + k] = 1.0
-                    pick[kind, 16 + 2 * i + k, x * C + k] = 1.0
     z2 = np.zeros((NZ, NZ), np.float32)
     z1 = np.zeros((NZ, NZ), np.float32)
     for z in range(NZ):
@@ -90,25 +82,32 @@
     upper = waves.astype(ml_dtypes.bfloat16)
     lower = (waves - upper.astype(np.float32)).astype(ml_dtypes.bfloat16)
     half = ml_dtypes.bfloat16
-    parts = [y2, y1, *cross, z2, z1, 3.0 * z1, *pick]
+    parts = [*y2, *y1, *cross, z2, z1, 3.0 * z1]
     parts = [np.pad(part, ((0, 0), (0, 256 - part.shape[1]))).astype(half) for part in parts]
     return np.concatenate(parts + [np.concatenate([upper, lower], axis=1)])
 
 
-AT_Y2, AT_Y1, AT_CROSS, AT_Z2, AT_Z1, AT_Z3 = 0, 128, 256, 640, 896, 1152
-AT_PICK, AT_WAVES, TABLE = 1408, 1504, 1760
-SHORT = AT_PICK
+AT_Y2, AT_Y1, AT_CROSS, AT_Z2, AT_Z1, AT_Z3 = 0, 384, 768, 1152, 1408, 1664
+AT_WAVES, TABLE = 1920, 2176
+SHORT = AT_WAVES
 
 
 def matrices(table, kind):
+    def part(at):
+        return table[pl.ds(pl.multiple_of(at + ROWS * kind, ROWS), ROWS)]
+
     return (
-        table[AT_Y2 : AT_Y2 + ROWS, : ROWS + 32],
-        table[AT_Y1 : AT_Y1 + ROWS, : ROWS + 32],
-        table[pl.ds(pl.multiple_of(AT_CROSS + ROWS * kind, ROWS), ROWS)],
+        part(AT_Y2)[:, : ROWS + 32],
+        part(AT_Y1)[:, : ROWS + 32],
+        part(AT_CROSS),
         table[AT_Z2 : AT_Z2 + NZ],
         table[AT_Z1 : AT_Z1 + NZ],
         table[AT_Z3 : AT_Z3 + NZ],
     )
+
+
+def rows_at(g):
+    return pl.ds(pl.multiple_of(g * ROWS, ROWS), ROWS)
 
 
 def dot(a, b):
@@ -182,8 +181,10 @@
     table_hbm, offsets_hbm, levels_hbm, moduli_hbm, old_hbm, now_hbm,
     last_hbm, prior_hbm, half_hbm, side_hbm, corner_hbm, spread_hbm,
     field, mod, half, side_out, side_in, corner, hot, gathered, basis, spread,
+    depth_hot, part_out, part_in,
     table, slot_tile, zbuf, ebuf, dbuf, kbuf,
     load_sem, store_sem, group_sem, send_sem, recv_sem, gsend_sem, grecv_sem,
+    slot_sem, rsend_sem, rrecv_sem,
 ):
     gx = lax.axis_index("gx")
     gy = lax.axis_index("gy")
@@ -196,15 +197,14 @@
         pltpu.make_async_copy(now_hbm, field.at[0], load_sem.at[0]),
         pltpu.make_async_copy(old_hbm, field.at[1], load_sem.at[1]),
         pltpu.make_async_copy(moduli_hbm, mod, load_sem.at[2]),
-        pltpu.make_async_copy(
-            offsets_hbm.at[pl.ds(pl.multiple_of(device // 4 * 8, 8), 8)], slot_tile.at[0], load_sem.at[3]
-        ),
-        pltpu.make_async_copy(
-            levels_hbm.at[pl.ds(pl.multiple_of(device // 4 * 8, 8), 8)], slot_tile.at[1], load_sem.at[4]
-        ),
-        pltpu.make_async_copy(table_hbm, table, load_sem.at[5]),
+        pltpu.make_async_copy(table_hbm, table, load_sem.at[3]),
     ]
-    for load in loads:
+    slot_loads = []
+    for x in range(4):
+        at = pl.ds(pl.multiple_of(x * 64 + pz * 16 + py // 2 * 8, 8), 8)
+        for k, ref in enumerate((offsets_hbm, levels_hbm)):
+            slot_loads.append(pltpu.make_async_copy(ref.at[at], slot_tile.at[k, x], slot_sem.at[k, x]))
+    for load in loads[:1] + slot_loads + loads[3:] + loads[1:3]:
         load.start()
 
     for p in range(2):
@@ -234,20 +234,16 @@
         def _():
             pl.semaphore_signal(barrier, inc=1, device_id=(gx + dx, gy + dy), device_id_type=MESH)
 
-    def ring_y(k):
-        return (gx, (py + k) % 4 * 2 + core)
-
-    def ring_z(k):
-        return (px * 4 + (pz + k) % 4, gy)
-
-    def ring_x(k):
-        return ((px + k) % 4 * 4 + pz, gy)
-
-    for ring in (ring_y, ring_z, ring_x):
-        for k in (1, 2, 3):
-            pl.semaphore_signal(barrier, inc=1, device_id=ring(k), device_id_type=MESH)
-    twin = (gx, py * 2 + 1 - core)
-    pl.semaphore_signal(barrier, inc=1, device_id=twin, device_id_type=MESH)
+    def in_plane(k):
+        return (px * 4 + (pz + k // 4) % 4, (py + k % 4) % 4 * 2 + core)
+
+    def owner(k):
+        return ((px + k // 2) % 4 * 4 + pz, py * 2 + (core + k) % 2)
+
+    for k in range(1, 16):
+        pl.semaphore_signal(barrier, inc=1, device_id=in_plane(k), device_id_type=MESH)
+    for k in range(1, 8):
+        pl.semaphore_signal(barrier, inc=1, device_id=owner(k), device_id_type=MESH)
 
     rows = lax.broadcasted_iota(jnp.int32, (8, 128), 0) + block * 8
     wavenum = (rows.astype(F32) + 0.5) * (4.0 / NK)
@@ -298,43 +294,34 @@
         return fresh_re, fresh_im
 
     lax.fori_loop(0, ND, upward, (zero, zero), unroll=4)
-    loads[5].wait()
+    loads[3].wait()
     product = dot(kbuf[...].reshape(ND * 8, 2 * F).astype(BF), table[AT_WAVES : AT_WAVES + 2 * F])
     product = product[:, :128] + product[:, 128:]
     lane = lax.broadcasted_iota(jnp.int32, (8, 128), 1) % ND
     mine = zero
     for d in range(ND):
         mine = jnp.where(lane == d, product[8 * d : 8 * d + 8], mine)
-    gathered[block] = mine
-
-    count = 10
+    seat = pz * 4 + py
+    gathered[seat] = mine
+
+    count = 22
     for dx, dy in steps:
         count = count + exists(dx, dy).astype(jnp.int32)
     pl.semaphore_wait(barrier, count)
 
-    def stage(index, ring, start, size):
-        copies = []
-        for k in (1, 2, 3):
-            piece = gathered.at[pl.ds(start, size)]
-            copies.append(
-                pltpu.make_async_remote_copy(
-                    src_ref=piece,
-                    dst_ref=piece,
-                    send_sem=gsend_sem.at[3 * index + k - 1],
-                    recv_sem=grecv_sem.at[3 * index + k - 1],
-                    device_id=ring(k),
-                    device_id_type=MESH,
-                )
-            )
-        for copy in copies:
-            copy.start()
-        return copies
-
-    def finish(copies):
-        for copy in copies:
-            copy.wait()
-
-    stage_y = stage(0, ring_y, block, 1)
+    gathers = [
+        pltpu.make_async_remote_copy(
+            src_ref=gathered.at[seat],
+            dst_ref=gathered.at[seat],
+            send_sem=gsend_sem.at[k],
+            recv_sem=grecv_sem.at[k],
+            device_id=in_plane(k),
+            device_id_type=MESH,
+        )
+        for k in range(1, 16)
+    ]
+    for copy in gathers:
+        copy.start()
 
     batches = [(6, 2), (0, 3), (3, 3)]
 
@@ -396,13 +383,18 @@
         p = n % 2
 
         def one_tile(g, carry):
-            kind = kind_of(g)
-            x = jnp.where(g == 0, 0, jnp.where(g == GROUPS - 1, C - 6, g * XG - 1))
-            pick = table[pl.ds(pl.multiple_of(AT_PICK + 32 * kind, 32), 32), : 6 * C]
+            x = jnp.where(g == 0, 0, jnp.where(g == GROUPS - 1, C - 8, g * XG - 1))
+            place = lax.broadcasted_iota(jnp.int32, (8, NZ), 0)
             for c in range(3):
-                tile = dot(pick, half[p, c, pl.ds(x + 2, 6)].reshape(6 * C, NZ)).astype(BF)
-                side_out[p, 0, g, c] = tile[:16]
-                side_out[p, 1, g, c] = tile[16:]
+                for s, y in ((0, C - 2), (1, 0)):
+                    rows = [jnp.zeros((8, NZ), F32)] * 2
+                    for i in range(8):
+                        at = pl.multiple_of((x + i) * C + y // 8 * 8, 8)
+                        tile = field[p, c, pl.ds(at, 8)]
+                        for k in range(2):
+                            line = jnp.broadcast_to(tile[y % 8 + k : y % 8 + k + 1], (8, NZ))
+                            rows[k] = jnp.where(place == i, line, rows[k])
+                    side_out[p, s, g, c] = below(*rows).astype(BF)
             return carry
 
         lax.fori_loop(first, first + size, one_tile, 0)
@@ -457,10 +449,10 @@
             [side_in[p, 1, g, c] for c in range(3)],
             [corner[p, kind, 0, c] for c in range(2)],
             [corner[p, kind, 1, c] for c in range(2)],
-            [field[p, c, pl.ds(x, XG)].reshape(ROWS, NZ) for c in range(3)],
-            [field[1 - p, c, pl.ds(x, XG)].reshape(ROWS, NZ) for c in range(3)],
-            mod[0, pl.ds(x, XG)].reshape(ROWS, NZ),
-            mod[1, pl.ds(x, XG)].reshape(ROWS, NZ),
+            [field[p, c, rows_at(g)] for c in range(3)],
+            [field[1 - p, c, rows_at(g)] for c in range(3)],
+            mod[0, rows_at(g)],
+            mod[1, rows_at(g)],
             sources,
             *matrices(table, kind),
         )
@@ -470,15 +462,13 @@
         return [values[ROWS * c : ROWS * c + ROWS] for c in range(3)]
 
     def keep(n, g, c, fresh):
-        x = g * XG
-        fresh = fresh.reshape(XG, C, NZ)
-        field[n % 2, c, pl.ds(x, XG)] = fresh
-        half[n % 2, c, pl.ds(x + 2, XG)] = fresh.astype(BF)
+        field[n % 2, c, rows_at(g)] = fresh
+        half[n % 2, c, pl.ds(g * XG + 2, XG)] = fresh.astype(BF).reshape(XG, C, NZ)
 
     def to_half(g, carry):
         x = g * XG
         for c in range(3):
-            half[0, c, pl.ds(x + 2, XG)] = field[0, c, pl.ds(x, XG)].astype(BF)
+            half[0, c, pl.ds(x + 2, XG)] = field[0, c, rows_at(g)].astype(BF).reshape(XG, C, NZ)
         return carry
 
     loads[0].wait()
@@ -486,24 +476,58 @@
     start(0, 0, 1, 2, 3, 4, 5)
     fill(0, 0, GROUPS)
     start(0, 6, 7, 8, 9, 10, 11)
-    finish(stage_y)
-    stage_z = stage(1, ring_z, block // 4 * 4, 4)
-
-    loads[3].wait()
-    loads[4].wait()
-    row = device % 4 * 2
+
+    for load in slot_loads:
+        load.wait()
+    first_row = py % 2 * 4
     mask = NK * NR // 2 - 1
-    for h in range(2):
-        part = pl.ds(128 * h, 128)
-        q = lane_spread(slot_tile[0, pl.ds(row + h, 1)])
-        lanes = lax.broadcasted_iota(jnp.int32, (128, 128), 1)
-        for b in range(NK // 128):
-            turns = (2 * (lanes + 128 * b) + 1) * q
-            turns = ((turns + (mask + 1) // 2) & mask) - (mask + 1) // 2
-            s = sine(turns.astype(F32) * (math.pi / (mask + 1)))
-            basis[part, 128 * b : 128 * b + 128] = (1.0 - 2.0 * s * s).astype(BF)
-    finish(stage_z)
-    stage_x = stage(2, ring_x, block // 16 * 16, 16)
+    across = lax.broadcasted_iota(jnp.int32, (128, 128), 1)
+    along = lax.broadcasted_iota(jnp.int32, (128, 128), 0)
+    odd_index = 2 * (along + (core * 4 + px) * 128) + 1
+
+    def cosines(t, carry):
+        q = slot_tile[0, t // 4, pl.ds(first_row + t % 4, 1)]
+        turns = odd_index * q
+        turns = ((turns + (mask + 1) // 2) & mask) - (mask + 1) // 2
+        s = sine(turns.astype(F32) * (math.pi / (mask + 1)))
+        basis[t] = (1.0 - 2.0 * s * s).astype(BF)
+        return carry
+
+    lax.fori_loop(0, 16, cosines, 0)
+    for copy in gathers:
+        copy.wait()
+    total = jnp.transpose(gathered[...].reshape(128, 128))
+    upper = total.astype(BF)
+    lower = (total - upper.astype(F32)).astype(BF)
+    both = beside(upper, lower)
+
+    def partial(u, carry):
+        cos = beside(basis[2 * u], basis[2 * u + 1])
+        sums = dot(both, below(cos, cos))
+        row = first_row + u % 2 * 2
+        level = beside(*[slot_tile[1, u // 2, pl.ds(row + h, 1)] for h in range(2)])
+        depth = lax.broadcasted_iota(jnp.int32, (STEPS * ND, Q), 0) % ND
+        sums = jnp.where(depth == level, sums, 0.0).reshape(STEPS, ND, Q)
+        sums = jnp.sum(sums, axis=1)
+        part_out[u] = below(sums[:, :128], sums[:, 128:])
+        return carry
+
+    lax.fori_loop(0, 8, partial, 0)
+    returns = []
+    for k in range(1, 8):
+        to = (px + k // 2) % 4 * 2 + (core + k) % 2
+        returns.append(
+            pltpu.make_async_remote_copy(
+                src_ref=part_out.at[to],
+                dst_ref=part_in.at[k],
+                send_sem=rsend_sem.at[k],
+                recv_sem=rrecv_sem.at[k],
+                device_id=owner(k),
+                device_id_type=MESH,
+            )
+        )
+    for copy in returns:
+        copy.start()
 
     def build_hot(g, carry):
         ids = lax.broadcasted_iota(jnp.int32, (ROWS, Q), 0) + g * ROWS
@@ -514,66 +538,27 @@
         return carry
 
     lax.fori_loop(0, GROUPS, build_hot, 0)
+    for h in range(2):
+        depth = lane_spread(target_ref[:, 128 * h : 128 * h + 128] % NZ)
+        for b in range(2):
+            depth_hot[128 * h : 128 * h + 128, 128 * b : 128 * b + 128] = jnp.where(
+                across + 128 * b == depth, 1.0, 0.0
+            ).astype(BF)
+    for copy in returns:
+        copy.wait()
+    traces = part_out[px * 2 + core]
+    for k in range(1, 8):
+        traces = traces + part_in[k]
+    slot = lax.broadcasted_iota(jnp.int32, (8, 128), 1) + lax.broadcasted_iota(jnp.int32, (8, 128), 0) // 4 * 128
+    traces = jnp.where(slot < live_ref[0], traces, 0.0)
+    for h in range(2):
+        part = slice(128 * h, 128 * h + 128)
+        for n in range(STEPS):
+            line = jnp.broadcast_to(traces[4 * h + n : 4 * h + n + 1], (128, 128))
+            diagonal = jnp.where(along == across, line, 0.0).astype(BF)
+            spread[n, part] = dot(diagonal, depth_hot[part]).astype(BF)
     loads[1].wait()
     loads[2].wait()
-    whole = gathered.at[pl.ds(core * 64, 64)]
-    swap = pltpu.make_async_remote_copy(
-        src_ref=whole,
-        dst_ref=whole,
-        send_sem=gsend_sem.at[9],
-        recv_sem=grecv_sem.at[9],
-        device_id=twin,
-        device_id_type=MESH,
-    )
-
-    def first_step(i, carry):
-        receive(0, i)
-
-        @pl.when(i == 4)
-        def _():
-            finish(stage_x)
-            swap.start()
-
-        g = group_at(i)
-        result = update(0, g, None)
-        for c in range(3):
-            field[1, c, pl.ds(g * XG, XG)] = result[c].reshape(XG, C, NZ)
-        return carry
-
-    lax.fori_loop(0, GROUPS, first_step, 0)
-    swap.wait()
-
-    total = gathered[...].reshape(NK, 128)
-    upper = total.astype(BF)
-    lower = (total - upper.astype(F32)).astype(BF)
-    picked = dot(basis[...], jnp.concatenate([upper, lower], axis=1))
-    picked = picked[:, :128] + picked[:, 128:]
-    ones = jnp.ones((128, NZ), BF)
-    for h in range(2):
-        part = slice(128 * h, 128 * h + 128)
-        lanes = lax.broadcasted_iota(jnp.int32, (128, 128), 1)
-        ids = lax.broadcasted_iota(jnp.int32, (128, 128), 0) + 128 * h
-        level = lane_spread(slot_tile[1, pl.ds(row + h, 1)])
-        live = jnp.logical_and(lanes % ND == level, ids < live_ref[0])
-        chosen = jnp.where(live, picked[part], 0.0)
-        depth = lane_spread(target_ref[:, 128 * h : 128 * h + 128] % NZ)
-        for n in range(STEPS):
-            values = dot(jnp.where(lanes // ND == n, chosen, 0.0).astype(BF), ones)
-            for b in range(2):
-                same = lanes + 128 * b == depth
-                spread[n, part, 128 * b : 128 * b + 128] = jnp.where(
-                    same, values[:, 128 * b : 128 * b + 128], 0.0
-                ).astype(BF)
-
-    def first_sources(i, carry):
-        g = group_at(i)
-        sources = injected(0, g)
-        for c in range(3):
-            keep(1, g, c, field[1, c, pl.ds(g * XG, XG)].reshape(ROWS, NZ) + sources[c])
-        publish(1, i)
-        return carry
-
-    lax.fori_loop(0, GROUPS, first_sources, 0)
 
     spread_store = pltpu.make_async_copy(spread.at[STEPS - 1], spread_hbm, store_sem.at[0])
     spread_store.start()
@@ -583,15 +568,16 @@
         x = g * XG
         return (
             pltpu.make_async_copy(
-                field.at[1, :, pl.ds(x, XG)], last_hbm.at[:, pl.ds(x, XG)], group_sem.at[0, g]
+                field.at[1, :, rows_at(g)], last_hbm.at[:, rows_at(g)], group_sem.at[0, g]
             ),
             pltpu.make_async_copy(
                 half.at[1, :, pl.ds(x + 2, XG)], half_hbm.at[:, pl.ds(x + 2, XG)], group_sem.at[1, g]
             ),
         )
 
-    for n in range(1, STEPS - 1):
-        sent(n - 1)
+    for n in range(STEPS - 1):
+        if n > 0:
+            sent(n - 1)
         if n == STEPS - 2:
             prior_store.start()
 
@@ -660,7 +646,7 @@
         return pltpu.make_async_copy(half_hbm.at[:, pl.ds(x, XG)], half.at[:, pl.ds(x, XG)], half_sem.at[k])
 
     def group_loads(g):
-        part = pl.ds(g * XG, XG)
+        part = rows_at(g)
         return [
             pltpu.make_async_copy(source.at[:, part], target.at[:, part], load_sem.at[k, g])
             for k, (source, target) in enumerate(
@@ -669,7 +655,7 @@
         ]
 
     def group_stores(g):
-        part = pl.ds(g * XG, XG)
+        part = rows_at(g)
         return [
             pltpu.make_async_copy(source.at[:, part], target.at[:, part], store_sem.at[k, g])
             for k, (source, target) in enumerate(((final, final_hbm), (now, copy_hbm)))
@@ -708,15 +694,15 @@
             [side[1, g, c] for c in range(3)],
             [corner[kind, 0, c] for c in range(2)],
             [corner[kind, 1, c] for c in range(2)],
-            [now[c, pl.ds(x, XG)].reshape(ROWS, NZ) for c in range(3)],
-            [before[c, pl.ds(x, XG)].reshape(ROWS, NZ) for c in range(3)],
-            mod[0, pl.ds(x, XG)].reshape(ROWS, NZ),
-            mod[1, pl.ds(x, XG)].reshape(ROWS, NZ),
+            [now[c, rows_at(g)] for c in range(3)],
+            [before[c, rows_at(g)] for c in range(3)],
+            mod[0, rows_at(g)],
+            mod[1, rows_at(g)],
             [values[ROWS * c : ROWS * c + ROWS] for c in range(3)],
             *matrices(table, kind),
         )
         for c in range(3):
-            final[c, pl.ds(x, XG)] = result[c].reshape(XG, C, NZ)
+            final[c, rows_at(g)] = result[c]
         stores[0].start()
         return carry
 
@@ -739,7 +725,10 @@
     vmem = pl.BlockSpec(memory_space=pltpu.VMEM)
     any_space = pl.BlockSpec(memory_space=pl.ANY)
     target = slot_target.reshape(1, Q)
-    block = jax.ShapeDtypeStruct((3, C, C, NZ), F32)
+    block = jax.ShapeDtypeStruct((3, C * C, NZ), F32)
+    whole = (3, C, C, NZ)
+    moduli = moduli.reshape(2, C * C, NZ)
+    field_old, field_now = field_old.reshape(block.shape), field_now.reshape(block.shape)
     dma = pltpu.SemaphoreType.DMA
     last, prior, half, side, corner, spread = pl.pallas_call(
         main_kernel,
@@ -754,29 +743,35 @@
         in_specs=[smem] * 5 + [vmem] + [any_space] * 6,
         out_specs=[any_space] * 6,
         scratch_shapes=[
-            pltpu.VMEM((2, 3, C, C, NZ), F32),
-            pltpu.VMEM((2, C, C, NZ), F32),
+            pltpu.VMEM((2, 3, C * C, NZ), F32),
+            pltpu.VMEM((2, C * C, NZ), F32),
             pltpu.VMEM((2, 3, C + 4, C, NZ), BF),
             pltpu.VMEM((2, 2, GROUPS, 3, 16, NZ), BF),
             pltpu.VMEM((2, 2, GROUPS, 3, 16, NZ), BF),
             pltpu.VMEM((2, 3, 2, 2, 16, NZ), BF),
             pltpu.VMEM((GROUPS, 3, ROWS, Q), BF),
-            pltpu.VMEM((NK // 8, 8, 128), F32),
-            pltpu.VMEM((Q, NK), BF),
+            pltpu.VMEM((16, 8, 128), F32),
+            pltpu.VMEM((16, 128, 128), BF),
             pltpu.VMEM((STEPS, Q, NZ), BF),
+            pltpu.VMEM((Q, NZ), BF),
+            pltpu.VMEM((8, 8, 128), F32),
+            pltpu.VMEM((8, 8, 128), F32),
             pltpu.VMEM((TABLE, NZ), BF),
-            pltpu.VMEM((2, 8, 128), jnp.int32),
+            pltpu.VMEM((2, 4, 8, 128), jnp.int32),
             pltpu.VMEM((ND + 1, 8, 128), F32),
             pltpu.VMEM((2, ND, 8, 128), F32),
             pltpu.VMEM((2, ND, 8, 128), F32),
             pltpu.VMEM((ND, 8, 2 * F), F32),
-            dma((6,)),
+            dma((4,)),
             dma((6,)),
             dma((2, GROUPS)),
             dma((STEPS, LINKS)),
             dma((STEPS, LINKS)),
-            dma((10,)),
-            dma((10,)),
+            dma((16,)),
+            dma((16,)),
+            dma((2, 4)),
+            dma((8,)),
+            dma((8,)),
         ],
         compiler_params=pltpu.CompilerParams(
             collective_id=0, has_side_effects=True, vmem_limit_bytes=VMEM
@@ -787,7 +782,7 @@
         slot_offset.reshape(Q, 128), slot_level.reshape(Q, 128), moduli, field_old, field_now,
     )
 
-    return pl.pallas_call(
+    final, copied = pl.pallas_call(
         last_kernel,
         out_shape=[block, block],
         in_specs=[vmem] + [any_space] * 8,
@@ -798,10 +793,10 @@
             pltpu.VMEM(side.shape, BF),
             pltpu.VMEM(corner.shape, BF),
             pltpu.VMEM(spread.shape, BF),
-            pltpu.VMEM((3, C, C, NZ), F32),
-            pltpu.VMEM((3, C, C, NZ), F32),
-            pltpu.VMEM((2, C, C, NZ), F32),
-            pltpu.VMEM((3, C, C, NZ), F32),
+            pltpu.VMEM(block.shape, F32),
+            pltpu.VMEM(block.shape, F32),
+            pltpu.VMEM(moduli.shape, F32),
+            pltpu.VMEM(block.shape, F32),
             dma((4,)),
             dma((GROUPS + 1,)),
             dma((3, GROUPS)),
@@ -809,6 +804,7 @@
         ],
         compiler_params=pltpu.CompilerParams(vmem_limit_bytes=VMEM),
     )(target, fixed, half, side, corner, spread, last, prior, moduli)
+    return final.reshape(whole), copied.reshape(whole)
 
 
 def solution(mesh):

time: 58.9 us -> 54.6 us (0.927)
  Pallas kernels: 57.5 us -> 53.1 us
    pallas_call x1, Pallas kernels: 49.2 us -> 45 us  [shards(): pl.pallas_call(main_kernel, out_shape=[block, block, jax.ShapeDtypeStruct...]
where the time goes in v2:
time: 54.6 us; the launch traced here: 54.4 us
  Pallas kernels  53.1 us (97%)
  between operations  1.29 us (2%)
    pallas_call x1, Pallas kernels, shards(): pl.pallas_call(main_kernel, out_shape=[block, block, jax.ShapeDtypeStruct...  45 us
    pallas_call x1, Pallas kernels, shards(): pl.pallas_call(last_kernel, out_shape=[block, block], in_specs=[vmem] + [...  8.18 us

profile of v2, /device:TPU:1, one launch (start us, length us, event | category | flops | bytes accessed | tf_op | source)
XLA Modules:
  0.0 54.4 jit_solution(10442253090999792374)
XLA Ops:
  1.3 45.0 %shard_map.131 = (f32[3,1024,256]{2,1,0:T(8,128)}, f32[3,1024,256]{2,1,0:T(8,128)}, bf16[3,36,32,256]{3,2,1,0:T(8,128)(2,1)}, bf16[2,8,3,16,256]{4,3,2,1,0:T(8,1...) custom-call(f32[8]{0:T(128)} %slow_ref.1, f32[8]{0:T(128)} %rigid_ref.1, f32[8]{0:T(128)} %damp_ref.1, ...), custom_call_target="tpu_custom_call" | custom-call | tf_op jit(solution)/shard_map/pallas_call | solution.py:733
  46.2 8.2 %shard_map.132 = (f32[3,1024,256]{2,1,0:T(8,128)}, f32[3,1024,256]{2,1,0:T(8,128)}) custom-call(s32[1,256]{1,0:T(1,128)} %bitcast.15, bf16[2176,256]{1,0:T(8,128)(2,1)} %constant.2.clone.table_hbm, bf16[3,36,32,256]{3,2,1,0:T(8,128)(2,1)} %get-tuple-element.10.half_hbm, bf16[2,8,3,16,256]{4,3,2,1,0:T(8,128)(2,1)} %get-tuple-element.11.side_hbm, ...), custom_call_target="tpu_custom_call" | custom-call | tf_op jit(solution)/shard_map/pallas_call | solution.py:785

commit v3 on v2

--- a/solution.py
+++ b/solution.py
@@ -24,7 +24,8 @@
 GROUPS = 8
 XG = 4
 ROWS = XG * C
-LINKS = 12
+SINGLES = 6
+LINKS = 6 + 2 * (SINGLES + 1)
 VMEM = 63 * 1024 * 1024
 MESH = pl.DeviceIdType.MESH
 BF = jnp.bfloat16
@@ -110,6 +111,18 @@
     return pl.ds(pl.multiple_of(g * ROWS, ROWS), ROWS)
 
 
+def group_at(i):
+    return jnp.where(i % 2 == 0, GROUPS - 1 - i // 2, i // 2)
+
+
+def place_of(g):
+    return jnp.where(g < GROUPS // 2, 2 * g + 1, 2 * (GROUPS - 1 - g))
+
+
+def kind_of(g):
+    return jnp.where(g == 0, 0, jnp.where(g == GROUPS - 1, 2, 1))
+
+
 def dot(a, b):
     return jnp.dot(a, b, preferred_element_type=F32)
 
@@ -323,25 +336,7 @@
     for copy in gathers:
         copy.start()
 
-    batches = [(6, 2), (0, 3), (3, 3)]
-
-    def message(n, index):
-        p = n % 2
-        if index < 2:
-            move = (1, 0) if index == 0 else (-1, 0)
-            source = half.at[p, :, pl.ds(C if index == 0 else 2, 2)]
-            target = half.at[p, :, pl.ds(0 if index == 0 else C + 2, 2)]
-        elif index < 6:
-            move = (1 if index < 4 else -1, 1 if index % 2 == 0 else -1)
-            source = half.at[
-                p, pl.ds(0, 2), C + 1 if move[0] == 1 else 2, pl.ds(16 if move[1] == 1 else 0, 16)
-            ]
-            target = corner.at[p, 0 if move[0] == 1 else 2, 0 if move[1] == 1 else 1]
-        else:
-            s, (first, size) = (index - 6) // 3, batches[(index - 6) % 3]
-            move = (0, 1) if s == 0 else (0, -1)
-            source = side_out.at[p, s, pl.ds(first, size)]
-            target = side_in.at[p, s, pl.ds(first, size)]
+    def send(n, move, source, target, index):
         copy = pltpu.make_async_remote_copy(
             src_ref=source,
             dst_ref=target,
@@ -352,92 +347,114 @@
         )
         return copy, exists(*move), exists(-move[0], -move[1])
 
-    def start(n, *indices):
-        for index in indices:
-            copy, there, _ = message(n, index)
+    def message(n, index):
+        p = n % 2
+        if index < 2:
+            move = (1, 0) if index == 0 else (-1, 0)
+            source = half.at[p, :, pl.ds(C if index == 0 else 2, 2)]
+            target = half.at[p, :, pl.ds(0 if index == 0 else C + 2, 2)]
+        else:
+            move = (1 if index < 4 else -1, 1 if index % 2 == 0 else -1)
+            source = half.at[
+                p, pl.ds(0, 2), C + 1 if move[0] == 1 else 2, pl.ds(16 if move[1] == 1 else 0, 16)
+            ]
+            target = corner.at[p, 0 if move[0] == 1 else 2, 0 if move[1] == 1 else 1]
+        return send(n, move, source, target, index)
+
+    def tiles(n, i, size):
+        return [
+            send(
+                n,
+                (0, 1) if s == 0 else (0, -1),
+                side_out.at[n % 2, s, pl.ds(i, size)],
+                side_in.at[n % 2, s, pl.ds(i, size)],
+                6 + (SINGLES + 1) * s + i,
+            )
+            for s in range(2)
+        ]
+
+    def start(messages):
+        for copy, there, _ in messages:
 
             @pl.when(there)
             def _():
                 copy.start()
 
-    def arrive(n, *indices):
-        for index in indices:
-            copy, _, here = message(n, index)
+    def arrive(messages):
+        for copy, _, here in messages:
 
             @pl.when(here)
             def _():
                 copy.wait_recv()
 
+    def everything(n):
+        return [message(n, index) for index in range(6)] + [
+            one for i in range(SINGLES + 1) for one in tiles(n, i, 1 if i < SINGLES else 2)
+        ]
+
     def sent(n):
-        for index in range(LINKS):
-            copy, there, _ = message(n, index)
+        for copy, there, _ in everything(n):
 
             @pl.when(there)
             def _():
                 copy.wait_send()
 
-    def kind_of(g):
-        return jnp.where(g == 0, 0, jnp.where(g == GROUPS - 1, 2, 1))
-
     def fill(n, first, size):
         p = n % 2
 
-        def one_tile(g, carry):
+        def one_tile(i, carry):
+            g = group_at(i)
             x = jnp.where(g == 0, 0, jnp.where(g == GROUPS - 1, C - 8, g * XG - 1))
             place = lax.broadcasted_iota(jnp.int32, (8, NZ), 0)
             for c in range(3):
                 for s, y in ((0, C - 2), (1, 0)):
                     rows = [jnp.zeros((8, NZ), F32)] * 2
-                    for i in range(8):
-                        at = pl.multiple_of((x + i) * C + y // 8 * 8, 8)
+                    for k in range(8):
+                        at = pl.multiple_of((x + k) * C + y // 8 * 8, 8)
                         tile = field[p, c, pl.ds(at, 8)]
-                        for k in range(2):
-                            line = jnp.broadcast_to(tile[y % 8 + k : y % 8 + k + 1], (8, NZ))
-                            rows[k] = jnp.where(place == i, line, rows[k])
-                    side_out[p, s, g, c] = below(*rows).astype(BF)
+                        for j in range(2):
+                            line = jnp.broadcast_to(tile[y % 8 + j : y % 8 + j + 1], (8, NZ))
+                            rows[j] = jnp.where(place == k, line, rows[j])
+                    side_out[p, s, i, c] = below(*rows).astype(BF)
             return carry
 
         lax.fori_loop(first, first + size, one_tile, 0)
-
-    def group_at(i):
-        return jnp.where(i < 3, GROUPS - 1 - i, i - 3)
 
     def publish(n, i):
         @pl.when(i == 0)
         def _():
-            start(n, 0, 2, 3)
-
-        @pl.when(i == 2)
-        def _():
-            fill(n, *batches[0])
-            start(n, 6, 9)
-
-        @pl.when(i == 3)
-        def _():
-            start(n, 1, 4, 5)
-
-        @pl.when(i == 6)
-        def _():
-            fill(n, *batches[1])
-            start(n, 7, 10)
-
-        @pl.when(i == 7)
-        def _():
-            fill(n, *batches[2])
-            start(n, 8, 11)
+            start([message(n, index) for index in (0, 2, 3)])
+
+        @pl.when(i == 1)
+        def _():
+            start([message(n, index) for index in (1, 4, 5)])
+
+        @pl.when(i >= 2)
+        def _():
+            fill(n, i - 2, 1)
+            start(tiles(n, i - 2, 1))
+
+        @pl.when(i == GROUPS - 1)
+        def _():
+            fill(n, SINGLES, 2)
+            start(tiles(n, SINGLES, 2))
 
     def receive(n, i):
         @pl.when(i == 0)
         def _():
-            arrive(n, 1, 4, 5, 6, 9)
-
-        @pl.when(i == 2)
-        def _():
-            arrive(n, 8, 11)
-
-        @pl.when(i == 3)
-        def _():
-            arrive(n, 0, 2, 3, 7, 10)
+            arrive([message(n, index) for index in (1, 4, 5)])
+
+        @pl.when(i == 1)
+        def _():
+            arrive([message(n, index) for index in (0, 2, 3)])
+
+        @pl.when(i < SINGLES)
+        def _():
+            arrive(tiles(n, i, 1))
+
+        @pl.when(i == SINGLES)
+        def _():
+            arrive(tiles(n, SINGLES, 2))
 
     def update(n, g, sources):
         p = n % 2
@@ -445,8 +462,8 @@
         kind = kind_of(g)
         return advance(
             [half[p, c, pl.ds(x, XG + 4)] for c in range(3)],
-            [side_in[p, 0, g, c] for c in range(3)],
-            [side_in[p, 1, g, c] for c in range(3)],
+            [side_in[p, 0, place_of(g), c] for c in range(3)],
+            [side_in[p, 1, place_of(g), c] for c in range(3)],
             [corner[p, kind, 0, c] for c in range(2)],
             [corner[p, kind, 1, c] for c in range(2)],
             [field[p, c, rows_at(g)] for c in range(3)],
@@ -473,9 +490,9 @@
 
     loads[0].wait()
     lax.fori_loop(0, GROUPS, to_half, 0)
-    start(0, 0, 1, 2, 3, 4, 5)
+    start([message(0, index) for index in range(6)])
     fill(0, 0, GROUPS)
-    start(0, 6, 7, 8, 9, 10, 11)
+    start(everything(0)[6:])
 
     for load in slot_loads:
         load.wait()
@@ -494,25 +511,6 @@
         return carry
 
     lax.fori_loop(0, 16, cosines, 0)
-    for copy in gathers:
-        copy.wait()
-    total = jnp.transpose(gathered[...].reshape(128, 128))
-    upper = total.astype(BF)
-    lower = (total - upper.astype(F32)).astype(BF)
-    both = beside(upper, lower)
-
-    def partial(u, carry):
-        cos = beside(basis[2 * u], basis[2 * u + 1])
-        sums = dot(both, below(cos, cos))
-        row = first_row + u % 2 * 2
-        level = beside(*[slot_tile[1, u // 2, pl.ds(row + h, 1)] for h in range(2)])
-        depth = lax.broadcasted_iota(jnp.int32, (STEPS * ND, Q), 0) % ND
-        sums = jnp.where(depth == level, sums, 0.0).reshape(STEPS, ND, Q)
-        sums = jnp.sum(sums, axis=1)
-        part_out[u] = below(sums[:, :128], sums[:, 128:])
-        return carry
-
-    lax.fori_loop(0, 8, partial, 0)
     returns = []
     for k in range(1, 8):
         to = (px + k // 2) % 4 * 2 + (core + k) % 2
@@ -526,9 +524,6 @@
                 device_id_type=MESH,
             )
         )
-    for copy in returns:
-        copy.start()
-
     def build_hot(g, carry):
         ids = lax.broadcasted_iota(jnp.int32, (ROWS, Q), 0) + g * ROWS
         columns = target_ref[...] // NZ
@@ -544,6 +539,42 @@
             depth_hot[128 * h : 128 * h + 128, 128 * b : 128 * b + 128] = jnp.where(
                 across + 128 * b == depth, 1.0, 0.0
             ).astype(BF)
+    def sum_up():
+        for copy in gathers:
+            copy.wait()
+        total = jnp.transpose(gathered[...].reshape(128, 128))
+        upper = total.astype(BF)
+        lower = (total - upper.astype(F32)).astype(BF)
+        both = beside(upper, lower)
+
+        def partial(u, carry):
+            cos = beside(basis[2 * u], basis[2 * u + 1])
+            sums = dot(both, below(cos, cos))
+            row = first_row + u % 2 * 2
+            level = beside(*[slot_tile[1, u // 2, pl.ds(row + h, 1)] for h in range(2)])
+            depth = lax.broadcasted_iota(jnp.int32, (STEPS * ND, Q), 0) % ND
+            sums = jnp.where(depth == level, sums, 0.0).reshape(STEPS, ND, Q)
+            sums = jnp.sum(sums, axis=1)
+            part_out[u] = below(sums[:, :128], sums[:, 128:])
+            return carry
+
+        lax.fori_loop(0, 8, partial, 0)
+        for copy in returns:
+            copy.start()
+
+    loads[1].wait()
+    loads[2].wait()
+
+    def first_step(i, carry):
+        receive(0, i)
+        pl.when(i == 2)(sum_up)
+        g = group_at(i)
+        result = update(0, g, None)
+        for c in range(3):
+            field[1, c, rows_at(g)] = result[c]
+        return carry
+
+    lax.fori_loop(0, GROUPS, first_step, 0)
     for copy in returns:
         copy.wait()
     traces = part_out[px * 2 + core]
@@ -557,8 +588,16 @@
             line = jnp.broadcast_to(traces[4 * h + n : 4 * h + n + 1], (128, 128))
             diagonal = jnp.where(along == across, line, 0.0).astype(BF)
             spread[n, part] = dot(diagonal, depth_hot[part]).astype(BF)
-    loads[1].wait()
-    loads[2].wait()
+
+    def first_sources(i, carry):
+        g = group_at(i)
+        sources = injected(0, g)
+        for c in range(3):
+            keep(1, g, c, field[1, c, rows_at(g)] + sources[c])
+        publish(1, i)
+        return carry
+
+    lax.fori_loop(0, GROUPS, first_sources, 0)
 
     spread_store = pltpu.make_async_copy(spread.at[STEPS - 1], spread_hbm, store_sem.at[0])
     spread_store.start()
@@ -575,9 +614,8 @@
             ),
         )
 
-    for n in range(STEPS - 1):
-        if n > 0:
-            sent(n - 1)
+    for n in range(1, STEPS - 1):
+        sent(n - 1)
         if n == STEPS - 2:
             prior_store.start()
 
@@ -596,17 +634,17 @@
         lax.fori_loop(0, GROUPS, later_step, 0)
 
     last = STEPS - 1
-    arrive(last, 0, 1)
+    arrive([message(last, index) for index in (0, 1)])
     ends = [
         pltpu.make_async_copy(half.at[1, :, pl.ds(x, 2)], half_hbm.at[:, pl.ds(x, 2)], store_sem.at[k])
         for x, k in ((0, 2), (C + 2, 3))
     ]
     for store in ends:
         store.start()
-    arrive(last, 2, 3, 4, 5)
+    arrive([message(last, index) for index in (2, 3, 4, 5)])
     corner_store = pltpu.make_async_copy(corner.at[1], corner_hbm, store_sem.at[4])
     corner_store.start()
-    arrive(last, 6, 7, 8, 9, 10, 11)
+    arrive(everything(last)[6:])
     side_store = pltpu.make_async_copy(side_in.at[1], side_hbm, store_sem.at[5])
     side_store.start()
     sent(last - 1)
@@ -661,37 +699,44 @@
             for k, (source, target) in enumerate(((final, final_hbm), (now, copy_hbm)))
         ]
 
-    half_load(0).start()
-    for load in small:
-        load.start()
-
-    def begin(g, carry):
+    def begin(g):
         half_load(g + 1).start()
         for load in group_loads(g):
             load.start()
-        return carry
-
-    lax.fori_loop(0, GROUPS, begin, 0)
+
+    ahead = 3
+    half_load(0).start()
+    small[0].start()
+    begin(0)
+    for load in small[1:]:
+        load.start()
+    for g in range(1, ahead):
+        begin(g)
     half_load(0).wait()
     for load in small:
         load.wait()
 
     def group(g, carry):
         x = g * XG
+
+        @pl.when(g + ahead < GROUPS)
+        def _():
+            begin(g + ahead)
+
         half_load(g + 1).wait()
         for load in group_loads(g):
             load.wait()
         stores = group_stores(g)
         stores[1].start()
-        kind = jnp.where(g == 0, 0, jnp.where(g == GROUPS - 1, 2, 1))
+        kind = kind_of(g)
         ids = lax.broadcasted_iota(jnp.int32, (ROWS, Q), 0) + g * ROWS
         columns = target_ref[...] // NZ
         hot = [jnp.where(ids + c * C * C == columns, 1.0, 0.0).astype(BF) for c in range(3)]
         values = dot(below(*hot), spread[...])
         result = advance(
             [half[c, pl.ds(x, XG + 4)] for c in range(3)],
-            [side[0, g, c] for c in range(3)],
-            [side[1, g, c] for c in range(3)],
+            [side[0, place_of(g), c] for c in range(3)],
+            [side[1, place_of(g), c] for c in range(3)],
             [corner[kind, 0, c] for c in range(2)],
             [corner[kind, 1, c] for c in range(2)],
             [now[c, rows_at(g)] for c in range(3)],

time: 54.6 us -> 54 us (0.989)
  the two profiles are of different devices: /device:TPU:1 before, /device:TPU:3 now
where the time goes in v3:
time: 54 us; the launch traced here: 53.7 us
  Pallas kernels  52.5 us (97%)
  between operations  1.29 us (2%)
    pallas_call x1, Pallas kernels, shards(): pl.pallas_call(main_kernel, out_shape=[block, block, jax.ShapeDtypeStruct...  43.2 us
    pallas_call x1, Pallas kernels, shards(): pl.pallas_call(last_kernel, out_shape=[block, block], in_specs=[vmem] + [...  9.26 us

profile of v3, /device:TPU:3, one launch (start us, length us, event | category | flops | bytes accessed | tf_op | source)
XLA Modules:
  0.0 53.7 jit_solution(15190988289855079202)
XLA Ops:
  1.3 43.2 %shard_map.131 = (f32[3,1024,256]{2,1,0:T(8,128)}, f32[3,1024,256]{2,1,0:T(8,128)}, bf16[3,36,32,256]{3,2,1,0:T(8,128)(2,1)}, bf16[2,8,3,16,256]{4,3,2,1,0:T(8,1...) custom-call(f32[8]{0:T(128)} %slow_ref.1, f32[8]{0:T(128)} %rigid_ref.1, f32[8]{0:T(128)} %damp_ref.1, ...), custom_call_target="tpu_custom_call" | custom-call | tf_op jit(solution)/shard_map/pallas_call | solution.py:778
  44.5 9.3 %shard_map.132 = (f32[3,1024,256]{2,1,0:T(8,128)}, f32[3,1024,256]{2,1,0:T(8,128)}) custom-call(s32[1,256]{1,0:T(1,128)} %bitcast.15, bf16[2176,256]{1,0:T(8,128)(2,1)} %constant.2.clone.table_hbm, bf16[3,36,32,256]{3,2,1,0:T(8,128)(2,1)} %get-tuple-element.10.half_hbm, bf16[2,8,3,16,256]{4,3,2,1,0:T(8,128)(2,1)} %get-tuple-element.11.side_hbm, ...), custom_call_target="tpu_custom_call" | custom-call | tf_op jit(solution)/shard_map/pallas_call | solution.py:830

commit v4 on v3

--- a/solution.py
+++ b/solution.py
@@ -24,8 +24,9 @@
 GROUPS = 8
 XG = 4
 ROWS = XG * C
-SINGLES = 6
-LINKS = 6 + 2 * (SINGLES + 1)
+TILES = 4
+LINKS = 6 + 2 * TILES
+ORDER = (7, 0, 6, 5, 1, 4, 2, 3)
 VMEM = 63 * 1024 * 1024
 MESH = pl.DeviceIdType.MESH
 BF = jnp.bfloat16
@@ -35,34 +36,39 @@
 def constants():
     low, high = ROWS, ROWS + 16
 
-    def place(x, y, kind):
+    def place(x, y, half):
         if y < 0:
-            return low + 8 * (y + 2) + x + (0, 1, 4)[kind]
+            return low + 8 * (y + 2) + x + XG * half
         if y >= C:
-            return high + 8 * (y - C) + x + (0, 1, 4)[kind]
+            return high + 8 * (y - C) + x + XG * half
         return x * C + y
 
-    y2 = np.zeros((3, ROWS, ROWS + 32), np.float32)
-    y1 = np.zeros((3, ROWS, ROWS + 32), np.float32)
-    cross = np.zeros((3, ROWS, ROWS + 96), np.float32)
-    for kind in range(3):
+    y2 = np.zeros((2, ROWS, ROWS + 32), np.float32)
+    y1 = np.zeros((2, ROWS, ROWS + 32), np.float32)
+    for half in range(2):
         for x in range(XG):
             for y in range(C):
                 row = x * C + y
                 for shift, factor in ((-2, -1.0), (-1, 16.0), (1, 16.0), (2, -1.0)):
-                    y2[kind, row, place(x, y + shift, kind)] += factor
-                y1[kind, row, place(x, y + 1, kind)] += 1.0
-                y1[kind, row, place(x, y - 1, kind)] -= 1.0
-        cross[kind, :, :ROWS] = 3.0 * y1[kind, :, :ROWS]
-        cross[kind, :, ROWS + 64 :] = 3.0 * y1[kind, :, ROWS:]
+                    y2[half, row, place(x, y + shift, half)] += factor
+                y1[half, row, place(x, y + 1, half)] += 1.0
+                y1[half, row, place(x, y - 1, half)] -= 1.0
+    cross = np.zeros((4, ROWS, ROWS + 96), np.float32)
+    for kind in range(4):
+        half = kind // 2
+        cross[kind, :, :ROWS] = 3.0 * y1[half, :, :ROWS]
+        cross[kind, :, ROWS + 64 :] = 3.0 * y1[half, :, ROWS:]
         for x in range(XG):
             for y, beyond, sign in ((0, -1, -3.0), (C - 1, C, 3.0)):
                 for step in (-1, 1):
-                    outside = (kind == 0 and x + step < 0) or (kind == 2 and x + step >= XG)
-                    if outside:
-                        spot = ROWS + 32 + 15 if beyond < 0 else ROWS + 48
+                    if (half == 0 and x + step < 0) or (half == 1 and x + step >= XG):
+                        spot = ROWS + (32 if beyond < 0 else 48)
+                        if kind in (0, 3):
+                            spot += 15 if beyond < 0 else 0
+                        else:
+                            spot += (8 if beyond < 0 else 0) + (7 if half == 0 else 0)
                     else:
-                        spot = place(x + step, beyond, kind)
+                        spot = place(x + step, beyond, half)
                     cross[kind, x * C + y, spot] += sign * step
     z2 = np.zeros((NZ, NZ), np.float32)
     z1 = np.zeros((NZ, NZ), np.float32)
@@ -88,39 +94,47 @@
     return np.concatenate(parts + [np.concatenate([upper, lower], axis=1)])
 
 
-AT_Y2, AT_Y1, AT_CROSS, AT_Z2, AT_Z1, AT_Z3 = 0, 384, 768, 1152, 1408, 1664
-AT_WAVES, TABLE = 1920, 2176
+AT_Y2, AT_Y1, AT_CROSS, AT_Z2, AT_Z1, AT_Z3 = 0, 256, 512, 1024, 1280, 1536
+AT_WAVES, TABLE = 1792, 2048
 SHORT = AT_WAVES
 
 
-def matrices(table, kind):
-    def part(at):
-        return table[pl.ds(pl.multiple_of(at + ROWS * kind, ROWS), ROWS)]
+def matrices(table, g):
+    kind = jnp.where(g == 0, 0, jnp.where(g == GROUPS - 1, 3, 1 + g % 2))
+
+    def part(at, k):
+        return table[pl.ds(pl.multiple_of(at + ROWS * k, ROWS), ROWS)]
 
     return (
-        part(AT_Y2)[:, : ROWS + 32],
-        part(AT_Y1)[:, : ROWS + 32],
-        part(AT_CROSS),
+        part(AT_Y2, g % 2)[:, : ROWS + 32],
+        part(AT_Y1, g % 2)[:, : ROWS + 32],
+        part(AT_CROSS, kind),
         table[AT_Z2 : AT_Z2 + NZ],
         table[AT_Z1 : AT_Z1 + NZ],
         table[AT_Z3 : AT_Z3 + NZ],
     )
 
 
+def halo_tiles(side, g):
+    own = g // 2 + 1
+    other = own - 1 + 2 * (g % 2)
+    return (
+        [side[0, own, c] for c in range(3)],
+        [side[1, own, c] for c in range(3)],
+        [side[0, other, c] for c in range(2)],
+        [side[1, other, c] for c in range(2)],
+    )
+
+
 def rows_at(g):
     return pl.ds(pl.multiple_of(g * ROWS, ROWS), ROWS)
 
 
 def group_at(i):
-    return jnp.where(i % 2 == 0, GROUPS - 1 - i // 2, i // 2)
-
-
-def place_of(g):
-    return jnp.where(g < GROUPS // 2, 2 * g + 1, 2 * (GROUPS - 1 - g))
-
-
-def kind_of(g):
-    return jnp.where(g == 0, 0, jnp.where(g == GROUPS - 1, 2, 1))
+    g = ORDER[-1]
+    for k in range(GROUPS - 1):
+        g = jnp.where(i == k, ORDER[k], g)
+    return g
 
 
 def dot(a, b):
@@ -192,8 +206,8 @@
 def main_kernel(
     slow_ref, rigid_ref, damp_ref, level_ref, live_ref, target_ref,
     table_hbm, offsets_hbm, levels_hbm, moduli_hbm, old_hbm, now_hbm,
-    last_hbm, prior_hbm, half_hbm, side_hbm, corner_hbm, spread_hbm,
-    field, mod, half, side_out, side_in, corner, hot, gathered, basis, spread,
+    last_hbm, prior_hbm, half_hbm, side_hbm, spread_hbm,
+    field, mod, half, side_out, side_in, hot, gathered, basis, spread,
     depth_hot, part_out, part_in,
     table, slot_tile, zbuf, ebuf, dbuf, kbuf,
     load_sem, store_sem, group_sem, send_sem, recv_sem, gsend_sem, grecv_sem,
@@ -223,7 +237,6 @@
     for p in range(2):
         half[p, :, 0:2] = jnp.zeros((3, 2, C, NZ), BF)
         half[p, :, C + 2 : C + 4] = jnp.zeros((3, 2, C, NZ), BF)
-        corner[p] = jnp.zeros(corner.shape[1:], BF)
         for s in range(2):
             side_in[p, s] = jnp.zeros(side_in.shape[2:], BF)
 
@@ -358,17 +371,17 @@
             source = half.at[
                 p, pl.ds(0, 2), C + 1 if move[0] == 1 else 2, pl.ds(16 if move[1] == 1 else 0, 16)
             ]
-            target = corner.at[p, 0 if move[0] == 1 else 2, 0 if move[1] == 1 else 1]
+            target = side_in.at[p, 0 if move[1] == 1 else 1, 0 if move[0] == 1 else TILES + 1, pl.ds(0, 2)]
         return send(n, move, source, target, index)
 
-    def tiles(n, i, size):
+    def tiles(n, k):
         return [
             send(
                 n,
                 (0, 1) if s == 0 else (0, -1),
-                side_out.at[n % 2, s, pl.ds(i, size)],
-                side_in.at[n % 2, s, pl.ds(i, size)],
-                6 + (SINGLES + 1) * s + i,
+                side_out.at[n % 2, s, k],
+                side_in.at[n % 2, s, k + 1],
+                6 + TILES * s + k,
             )
             for s in range(2)
         ]
@@ -388,9 +401,7 @@
                 copy.wait_recv()
 
     def everything(n):
-        return [message(n, index) for index in range(6)] + [
-            one for i in range(SINGLES + 1) for one in tiles(n, i, 1 if i < SINGLES else 2)
-        ]
+        return [message(n, index) for index in range(6)] + [one for k in range(TILES) for one in tiles(n, k)]
 
     def sent(n):
         for copy, there, _ in everything(n):
@@ -399,26 +410,18 @@
             def _():
                 copy.wait_send()
 
-    def fill(n, first, size):
+    def fill(n, k):
         p = n % 2
-
-        def one_tile(i, carry):
-            g = group_at(i)
-            x = jnp.where(g == 0, 0, jnp.where(g == GROUPS - 1, C - 8, g * XG - 1))
-            place = lax.broadcasted_iota(jnp.int32, (8, NZ), 0)
-            for c in range(3):
-                for s, y in ((0, C - 2), (1, 0)):
-                    rows = [jnp.zeros((8, NZ), F32)] * 2
-                    for k in range(8):
-                        at = pl.multiple_of((x + k) * C + y // 8 * 8, 8)
-                        tile = field[p, c, pl.ds(at, 8)]
-                        for j in range(2):
-                            line = jnp.broadcast_to(tile[y % 8 + j : y % 8 + j + 1], (8, NZ))
-                            rows[j] = jnp.where(place == k, line, rows[j])
-                    side_out[p, s, i, c] = below(*rows).astype(BF)
-            return carry
-
-        lax.fori_loop(first, first + size, one_tile, 0)
+        place = lax.broadcasted_iota(jnp.int32, (8, NZ), 0)
+        for c in range(3):
+            for s, y in ((0, C - 2), (1, 0)):
+                rows = [jnp.zeros((8, NZ), F32)] * 2
+                for x in range(8):
+                    tile = field[p, c, pl.ds((8 * k + x) * C + y // 8 * 8, 8)]
+                    for j in range(2):
+                        line = jnp.broadcast_to(tile[y % 8 + j : y % 8 + j + 1], (8, NZ))
+                        rows[j] = jnp.where(place == x, line, rows[j])
+                side_out[p, s, k, c] = below(*rows).astype(BF)
 
     def publish(n, i):
         @pl.when(i == 0)
@@ -429,49 +432,42 @@
         def _():
             start([message(n, index) for index in (1, 4, 5)])
 
-        @pl.when(i >= 2)
-        def _():
-            fill(n, i - 2, 1)
-            start(tiles(n, i - 2, 1))
-
-        @pl.when(i == GROUPS - 1)
-        def _():
-            fill(n, SINGLES, 2)
-            start(tiles(n, SINGLES, 2))
+        for at, k in ((2, 3), (4, 0), (5, 2), (7, 1)):
+
+            @pl.when(i == at)
+            def _():
+                fill(n, k)
+                start(tiles(n, k))
 
     def receive(n, i):
         @pl.when(i == 0)
         def _():
-            arrive([message(n, index) for index in (1, 4, 5)])
+            arrive([message(n, index) for index in (1, 4, 5)] + tiles(n, 3))
 
         @pl.when(i == 1)
         def _():
-            arrive([message(n, index) for index in (0, 2, 3)])
-
-        @pl.when(i < SINGLES)
+            arrive([message(n, index) for index in (0, 2, 3)] + tiles(n, 0))
+
+        @pl.when(i == 2)
         def _():
-            arrive(tiles(n, i, 1))
-
-        @pl.when(i == SINGLES)
+            arrive(tiles(n, 2))
+
+        @pl.when(i == 4)
         def _():
-            arrive(tiles(n, SINGLES, 2))
+            arrive(tiles(n, 1))
 
     def update(n, g, sources):
         p = n % 2
         x = g * XG
-        kind = kind_of(g)
         return advance(
             [half[p, c, pl.ds(x, XG + 4)] for c in range(3)],
-            [side_in[p, 0, place_of(g), c] for c in range(3)],
-            [side_in[p, 1, place_of(g), c] for c in range(3)],
-            [corner[p, kind, 0, c] for c in range(2)],
-            [corner[p, kind, 1, c] for c in range(2)],
+            *halo_tiles(side_in.at[p], g),
             [field[p, c, rows_at(g)] for c in range(3)],
             [field[1 - p, c, rows_at(g)] for c in range(3)],
             mod[0, rows_at(g)],
             mod[1, rows_at(g)],
             sources,
-            *matrices(table, kind),
+            *matrices(table, g),
         )
 
     def injected(n, g):
@@ -491,8 +487,9 @@
     loads[0].wait()
     lax.fori_loop(0, GROUPS, to_half, 0)
     start([message(0, index) for index in range(6)])
-    fill(0, 0, GROUPS)
-    start(everything(0)[6:])
+    for k in range(TILES):
+        fill(0, k)
+        start(tiles(0, k))
 
     for load in slot_loads:
         load.wait()
@@ -641,15 +638,12 @@
     ]
     for store in ends:
         store.start()
-    arrive([message(last, index) for index in (2, 3, 4, 5)])
-    corner_store = pltpu.make_async_copy(corner.at[1], corner_hbm, store_sem.at[4])
-    corner_store.start()
-    arrive(everything(last)[6:])
+    arrive(everything(last)[2:])
     side_store = pltpu.make_async_copy(side_in.at[1], side_hbm, store_sem.at[5])
     side_store.start()
     sent(last - 1)
     sent(last)
-    for store in (spread_store, prior_store, *ends, corner_store, side_store):
+    for store in (spread_store, prior_store, *ends, side_store):
         store.wait()
 
     def drain(g, carry):
@@ -662,9 +656,9 @@
 
 def last_kernel(
     target_ref,
-    table_hbm, half_hbm, side_hbm, corner_hbm, spread_hbm, now_hbm, before_hbm, moduli_hbm,
+    table_hbm, half_hbm, side_hbm, spread_hbm, now_hbm, before_hbm, moduli_hbm,
     final_hbm, copy_hbm,
-    table, half, side, corner, spread, now, before, mod, final,
+    table, half, side, spread, now, before, mod, final,
     sem, half_sem, load_sem, store_sem,
 ):
     small = [
@@ -674,7 +668,6 @@
                 (table_hbm.at[pl.ds(0, SHORT)], table),
                 (spread_hbm, spread),
                 (side_hbm, side),
-                (corner_hbm, corner),
             )
         )
     ]
@@ -704,13 +697,12 @@
         for load in group_loads(g):
             load.start()
 
-    ahead = 3
     half_load(0).start()
     small[0].start()
     begin(0)
     for load in small[1:]:
         load.start()
-    for g in range(1, ahead):
+    for g in range(1, GROUPS):
         begin(g)
     half_load(0).wait()
     for load in small:
@@ -718,33 +710,25 @@
 
     def group(g, carry):
         x = g * XG
-
-        @pl.when(g + ahead < GROUPS)
-        def _():
-            begin(g + ahead)
 
         half_load(g + 1).wait()
         for load in group_loads(g):
             load.wait()
         stores = group_stores(g)
         stores[1].start()
-        kind = kind_of(g)
         ids = lax.broadcasted_iota(jnp.int32, (ROWS, Q), 0) + g * ROWS
         columns = target_ref[...] // NZ
         hot = [jnp.where(ids + c * C * C == columns, 1.0, 0.0).astype(BF) for c in range(3)]
         values = dot(below(*hot), spread[...])
         result = advance(
             [half[c, pl.ds(x, XG + 4)] for c in range(3)],
-            [side[0, place_of(g), c] for c in range(3)],
-            [side[1, place_of(g), c] for c in range(3)],
-            [corner[kind, 0, c] for c in range(2)],
-            [corner[kind, 1, c] for c in range(2)],
+            *halo_tiles(side, g),
             [now[c, rows_at(g)] for c in range(3)],
             [before[c, rows_at(g)] for c in range(3)],
             mod[0, rows_at(g)],
             mod[1, rows_at(g)],
             [values[ROWS * c : ROWS * c + ROWS] for c in range(3)],
-            *matrices(table, kind),
+            *matrices(table, g),
         )
         for c in range(3):
             final[c, rows_at(g)] = result[c]
@@ -775,25 +759,23 @@
     moduli = moduli.reshape(2, C * C, NZ)
     field_old, field_now = field_old.reshape(block.shape), field_now.reshape(block.shape)
     dma = pltpu.SemaphoreType.DMA
-    last, prior, half, side, corner, spread = pl.pallas_call(
+    last, prior, half, side, spread = pl.pallas_call(
         main_kernel,
         out_shape=[
             block,
             block,
             jax.ShapeDtypeStruct((3, C + 4, C, NZ), BF),
-            jax.ShapeDtypeStruct((2, GROUPS, 3, 16, NZ), BF),
-            jax.ShapeDtypeStruct((3, 2, 2, 16, NZ), BF),
+            jax.ShapeDtypeStruct((2, TILES + 2, 3, 16, NZ), BF),
             jax.ShapeDtypeStruct((Q, NZ), BF),
         ],
         in_specs=[smem] * 5 + [vmem] + [any_space] * 6,
-        out_specs=[any_space] * 6,
+        out_specs=[any_space] * 5,
         scratch_shapes=[
             pltpu.VMEM((2, 3, C * C, NZ), F32),
             pltpu.VMEM((2, C * C, NZ), F32),
             pltpu.VMEM((2, 3, C + 4, C, NZ), BF),
-            pltpu.VMEM((2, 2, GROUPS, 3, 16, NZ), BF),
-            pltpu.VMEM((2, 2, GROUPS, 3, 16, NZ), BF),
-            pltpu.VMEM((2, 3, 2, 2, 16, NZ), BF),
+            pltpu.VMEM((2, 2, TILES, 3, 16, NZ), BF),
+            pltpu.VMEM((2, 2, TILES + 2, 3, 16, NZ), BF),
             pltpu.VMEM((GROUPS, 3, ROWS, Q), BF),
             pltpu.VMEM((16, 8, 128), F32),
             pltpu.VMEM((16, 128, 128), BF),
@@ -830,25 +812,24 @@
     final, copied = pl.pallas_call(
         last_kernel,
         out_shape=[block, block],
-        in_specs=[vmem] + [any_space] * 8,
+        in_specs=[vmem] + [any_space] * 7,
         out_specs=[any_space] * 2,
         scratch_shapes=[
             pltpu.VMEM((SHORT, NZ), BF),
             pltpu.VMEM(half.shape, BF),
             pltpu.VMEM(side.shape, BF),
-            pltpu.VMEM(corner.shape, BF),
             pltpu.VMEM(spread.shape, BF),
             pltpu.VMEM(block.shape, F32),
             pltpu.VMEM(block.shape, F32),
             pltpu.VMEM(moduli.shape, F32),
             pltpu.VMEM(block.shape, F32),
-            dma((4,)),
+            dma((3,)),
             dma((GROUPS + 1,)),
             dma((3, GROUPS)),
             dma((2, GROUPS)),
         ],
         compiler_params=pltpu.CompilerParams(vmem_limit_bytes=VMEM),
-    )(target, fixed, half, side, corner, spread, last, prior, moduli)
+    )(target, fixed, half, side, spread, last, prior, moduli)
     return final.reshape(whole), copied.reshape(whole)
 
 

time: 54 us -> 54.4 us (level)
    pallas_call x1, Pallas kernels: 9.26 us -> 10.4 us  [shards(): pl.pallas_call(last_kernel, out_shape=[block, block], in_specs=[vmem] + [...]
    pallas_call x1, Pallas kernels: 43.2 us -> 42.5 us  [shards(): pl.pallas_call(main_kernel, out_shape=[block, block, jax.ShapeDtypeStruct...]
where the time goes in v4:
time: 54.4 us; the launch traced here: 54.3 us
  Pallas kernels  53 us (97%)
  between operations  1.29 us (2%)
    pallas_call x1, Pallas kernels, shards(): pl.pallas_call(main_kernel, out_shape=[block, block, jax.ShapeDtypeStruct...  42.5 us
    pallas_call x1, Pallas kernels, shards(): pl.pallas_call(last_kernel, out_shape=[block, block], in_specs=[vmem] + [...  10.4 us

profile of v4, /device:TPU:3, one launch (start us, length us, event | category | flops | bytes accessed | tf_op | source)
XLA Modules:
  0.0 54.3 jit_solution(8057047894428807612)
XLA Ops:
  1.3 42.5 %shard_map.131 = (f32[3,1024,256]{2,1,0:T(8,128)}, f32[3,1024,256]{2,1,0:T(8,128)}, bf16[3,36,32,256]{3,2,1,0:T(8,128)(2,1)}, bf16[2,6,3,16,256]{4,3,2,1,0:T(8,128)(2,1)}, bf16[256,256]{1,0:T(8,128)(2,1)}) custom-call(f32[8]{0:T(128)} %slow_ref.1, f32[8]{0:T(128)} %rigid_ref.1, f32[8]{0:T(128)} %damp_ref.1, s32[32]{0:T(128)} %level_ref.1, ...), custom_call_target="tpu_custom_call" | custom-call | tf_op jit(solution)/shard_map/pallas_call | solution.py:762
  43.8 10.4 %shard_map.132 = (f32[3,1024,256]{2,1,0:T(8,128)}, f32[3,1024,256]{2,1,0:T(8,128)}) custom-call(s32[1,256]{1,0:T(1,128)} %bitcast.15, bf16[2048,256]{1,0:T(8,128)(2,1)} %constant.2.clone.table_hbm, bf16[3,36,32,256]{3,2,1,0:T(8,128)(2,1)} %get-tuple-element.9.half_hbm, bf16[2,6,3,16,256]{4,3,2,1,0:T(8,128)(2,1)} %get-tuple-element.10.side_hbm, ...), custom_call_target="tpu_custom_call" | custom-call | tf_op jit(solution)/shard_map/pallas_call | solution.py:812

commit v5 on v4

--- a/solution.py
+++ b/solution.py
@@ -601,15 +601,11 @@
     prior_store = pltpu.make_async_copy(field.at[0], prior_hbm, store_sem.at[1])
 
     def last_stores(g):
-        x = g * XG
-        return (
+        return [
             pltpu.make_async_copy(
-                field.at[1, :, rows_at(g)], last_hbm.at[:, rows_at(g)], group_sem.at[0, g]
-            ),
-            pltpu.make_async_copy(
-                half.at[1, :, pl.ds(x + 2, XG)], half_hbm.at[:, pl.ds(x + 2, XG)], group_sem.at[1, g]
-            ),
-        )
+                field.at[1, :, rows_at(g)], last_hbm.at[:, rows_at(g)], group_sem.at[g]
+            )
+        ]
 
     for n in range(1, STEPS - 1):
         sent(n - 1)
@@ -633,7 +629,7 @@
     last = STEPS - 1
     arrive([message(last, index) for index in (0, 1)])
     ends = [
-        pltpu.make_async_copy(half.at[1, :, pl.ds(x, 2)], half_hbm.at[:, pl.ds(x, 2)], store_sem.at[k])
+        pltpu.make_async_copy(half.at[1, :, pl.ds(x, 2)], half_hbm.at[:, pl.ds(2 * k - 4, 2)], store_sem.at[k])
         for x, k in ((0, 2), (C + 2, 3))
     ]
     for store in ends:
@@ -659,7 +655,7 @@
     table_hbm, half_hbm, side_hbm, spread_hbm, now_hbm, before_hbm, moduli_hbm,
     final_hbm, copy_hbm,
     table, half, side, spread, now, before, mod, final,
-    sem, half_sem, load_sem, store_sem,
+    sem, load_sem, store_sem,
 ):
     small = [
         pltpu.make_async_copy(source, target, sem.at[k])
@@ -668,13 +664,11 @@
                 (table_hbm.at[pl.ds(0, SHORT)], table),
                 (spread_hbm, spread),
                 (side_hbm, side),
+                (half_hbm.at[:, pl.ds(0, 2)], half.at[:, pl.ds(0, 2)]),
+                (half_hbm.at[:, pl.ds(2, 2)], half.at[:, pl.ds(C + 2, 2)]),
             )
         )
     ]
-
-    def half_load(k):
-        x = k * XG
-        return pltpu.make_async_copy(half_hbm.at[:, pl.ds(x, XG)], half.at[:, pl.ds(x, XG)], half_sem.at[k])
 
     def group_loads(g):
         part = rows_at(g)
@@ -692,30 +686,36 @@
             for k, (source, target) in enumerate(((final, final_hbm), (now, copy_hbm)))
         ]
 
-    def begin(g):
-        half_load(g + 1).start()
+    for load in small:
+        load.start()
+
+    def begin_one(g, carry):
         for load in group_loads(g):
             load.start()
-
-    half_load(0).start()
-    small[0].start()
-    begin(0)
-    for load in small[1:]:
-        load.start()
-    for g in range(1, GROUPS):
-        begin(g)
-    half_load(0).wait()
+        return carry
+
+    lax.fori_loop(0, GROUPS, begin_one, 0)
     for load in small:
         load.wait()
 
+    def to_half(g):
+        for load in group_loads(g):
+            load.wait()
+        for c in range(3):
+            half[c, pl.ds(g * XG + 2, XG)] = now[c, rows_at(g)].astype(BF).reshape(XG, C, NZ)
+
+    to_half(0)
+
     def group(g, carry):
         x = g * XG
 
-        half_load(g + 1).wait()
-        for load in group_loads(g):
-            load.wait()
         stores = group_stores(g)
         stores[1].start()
+
+        @pl.when(g < GROUPS - 1)
+        def _():
+            to_half(g + 1)
+
         ids = lax.broadcasted_iota(jnp.int32, (ROWS, Q), 0) + g * ROWS
         columns = target_ref[...] // NZ
         hot = [jnp.where(ids + c * C * C == columns, 1.0, 0.0).astype(BF) for c in range(3)]
@@ -764,7 +764,7 @@
         out_shape=[
             block,
             block,
-            jax.ShapeDtypeStruct((3, C + 4, C, NZ), BF),
+            jax.ShapeDtypeStruct((3, 4, C, NZ), BF),
             jax.ShapeDtypeStruct((2, TILES + 2, 3, 16, NZ), BF),
             jax.ShapeDtypeStruct((Q, NZ), BF),
         ],
@@ -791,7 +791,7 @@
             pltpu.VMEM((ND, 8, 2 * F), F32),
             dma((4,)),
             dma((6,)),
-            dma((2, GROUPS)),
+            dma((GROUPS,)),
             dma((STEPS, LINKS)),
             dma((STEPS, LINKS)),
             dma((16,)),
@@ -816,15 +816,14 @@
         out_specs=[any_space] * 2,
         scratch_shapes=[
             pltpu.VMEM((SHORT, NZ), BF),
-            pltpu.VMEM(half.shape, BF),
+            pltpu.VMEM((3, C + 4, C, NZ), BF),
             pltpu.VMEM(side.shape, BF),
             pltpu.VMEM(spread.shape, BF),
             pltpu.VMEM(block.shape, F32),
             pltpu.VMEM(block.shape, F32),
             pltpu.VMEM(moduli.shape, F32),
             pltpu.VMEM(block.shape, F32),
-            dma((3,)),
-            dma((GROUPS + 1,)),
+            dma((5,)),
             dma((3, GROUPS)),
             dma((2, GROUPS)),
         ],

time: 54.4 us -> 52.2 us (0.960)
  Pallas kernels: 53 us -> 50.8 us
    pallas_call x1, Pallas kernels: 10.4 us -> 8.35 us  [shards(): pl.pallas_call(last_kernel, out_shape=[block, block], in_specs=[vmem] + [...]
where the time goes in v5:
time: 52.2 us; the launch traced here: 52.1 us
  Pallas kernels  50.8 us (97%)
  between operations  1.29 us (2%)
    pallas_call x1, Pallas kernels, shards(): pl.pallas_call(main_kernel, out_shape=[block, block, jax.ShapeDtypeStruct...  42.5 us
    pallas_call x1, Pallas kernels, shards(): pl.pallas_call(last_kernel, out_shape=[block, block], in_specs=[vmem] + [...  8.35 us

profile of v5, /device:TPU:3, one launch (start us, length us, event | category | flops | bytes accessed | tf_op | source)
XLA Modules:
  0.0 52.1 jit_solution(18286572200965083739)
XLA Ops:
  1.3 42.5 %shard_map.131 = (f32[3,1024,256]{2,1,0:T(8,128)}, f32[3,1024,256]{2,1,0:T(8,128)}, bf16[3,4,32,256]{3,2,1,0:T(8,128)(2,1)}, bf16[2,6,3,16,256]{4,3,2,1,0:T(8,128)(2,1)}, bf16[256,256]{1,0:T(8,128)(2,1)}) custom-call(f32[8]{0:T(128)} %slow_ref.1, f32[8]{0:T(128)} %rigid_ref.1, f32[8]{0:T(128)} %damp_ref.1, s32[32]{0:T(128)} %level_ref.1, ...), custom_call_target="tpu_custom_call" | custom-call | tf_op jit(solution)/shard_map/pallas_call | solution.py:762
  43.7 8.4 %shard_map.132 = (f32[3,1024,256]{2,1,0:T(8,128)}, f32[3,1024,256]{2,1,0:T(8,128)}) custom-call(s32[1,256]{1,0:T(1,128)} %bitcast.15, bf16[2048,256]{1,0:T(8,128)(2,1)} %constant.2.clone.table_hbm, bf16[3,4,32,256]{3,2,1,0:T(8,128)(2,1)} %get-tuple-element.9.half_hbm, bf16[2,6,3,16,256]{4,3,2,1,0:T(8,128)(2,1)} %get-tuple-element.10.side_hbm, ...), custom_call_target="tpu_custom_call" | custom-call | tf_op jit(solution)/shard_map/pallas_call | solution.py:812

commit v6 on v5

--- a/solution.py
+++ b/solution.py
@@ -26,7 +26,8 @@
 ROWS = XG * C
 TILES = 4
 LINKS = 6 + 2 * TILES
-ORDER = (7, 0, 6, 5, 1, 4, 2, 3)
+ORDER = (6, 5, 7, 0, 4, 1, 2, 3)
+ADDING = (7, 0, 6, 5, 4, 1, 2, 3)
 VMEM = 63 * 1024 * 1024
 MESH = pl.DeviceIdType.MESH
 BF = jnp.bfloat16
@@ -130,10 +131,10 @@
     return pl.ds(pl.multiple_of(g * ROWS, ROWS), ROWS)
 
 
-def group_at(i):
-    g = ORDER[-1]
+def group_at(i, order=ORDER):
+    g = order[-1]
     for k in range(GROUPS - 1):
-        g = jnp.where(i == k, ORDER[k], g)
+        g = jnp.where(i == k, order[k], g)
     return g
 
 
@@ -295,7 +296,7 @@
 
     one = jnp.ones((8, 128), F32)
     zero = jnp.zeros((8, 128), F32)
-    lax.fori_loop(0, ND, downward, (one, zero), unroll=4)
+    lax.fori_loop(0, ND, downward, (one, zero), unroll=8)
     zbuf[ND] = zbuf[ND - 1]
 
     def upward(step, carry):
@@ -423,38 +424,37 @@
                         rows[j] = jnp.where(place == x, line, rows[j])
                 side_out[p, s, k, c] = below(*rows).astype(BF)
 
-    def publish(n, i):
-        @pl.when(i == 0)
+    def publish(n, i, order=ORDER):
+        @pl.when(i == order.index(GROUPS - 1))
         def _():
             start([message(n, index) for index in (0, 2, 3)])
 
-        @pl.when(i == 1)
+        @pl.when(i == order.index(0))
         def _():
             start([message(n, index) for index in (1, 4, 5)])
 
-        for at, k in ((2, 3), (4, 0), (5, 2), (7, 1)):
-
-            @pl.when(i == at)
+        for k in range(TILES):
+
+            @pl.when(i == max(order.index(2 * k), order.index(2 * k + 1)))
             def _():
                 fill(n, k)
                 start(tiles(n, k))
 
     def receive(n, i):
-        @pl.when(i == 0)
+        @pl.when(i == ORDER.index(GROUPS - 1))
         def _():
-            arrive([message(n, index) for index in (1, 4, 5)] + tiles(n, 3))
-
-        @pl.when(i == 1)
+            arrive([message(n, index) for index in (1, 4, 5)])
+
+        @pl.when(i == ORDER.index(0))
         def _():
-            arrive([message(n, index) for index in (0, 2, 3)] + tiles(n, 0))
-
-        @pl.when(i == 2)
-        def _():
-            arrive(tiles(n, 2))
-
-        @pl.when(i == 4)
-        def _():
-            arrive(tiles(n, 1))
+            arrive([message(n, index) for index in (0, 2, 3)])
+
+        for k in range(TILES):
+            readers = [g for g in range(2 * k - 1, 2 * k + 3) if 0 <= g < GROUPS]
+
+            @pl.when(i == min(ORDER.index(g) for g in readers))
+            def _():
+                arrive(tiles(n, k))
 
     def update(n, g, sources):
         p = n % 2
@@ -587,11 +587,11 @@
             spread[n, part] = dot(diagonal, depth_hot[part]).astype(BF)
 
     def first_sources(i, carry):
-        g = group_at(i)
+        g = group_at(i, ADDING)
         sources = injected(0, g)
         for c in range(3):
             keep(1, g, c, field[1, c, rows_at(g)] + sources[c])
-        publish(1, i)
+        publish(1, i, ADDING)
         return carry
 
     lax.fori_loop(0, GROUPS, first_sources, 0)

time: 52.2 us -> 51.2 us (0.981)
  Pallas kernels: 50.8 us -> 49.7 us
    pallas_call x1, Pallas kernels: 42.5 us -> 41.4 us  [shards(): pl.pallas_call(main_kernel, out_shape=[block, block, jax.ShapeDtypeStruct...]
where the time goes in v6:
time: 51.2 us; the launch traced here: 51 us
  Pallas kernels  49.7 us (97%)
  between operations  1.29 us (3%)
    pallas_call x1, Pallas kernels, shards(): pl.pallas_call(main_kernel, out_shape=[block, block, jax.ShapeDtypeStruct...  41.4 us
    pallas_call x1, Pallas kernels, shards(): pl.pallas_call(last_kernel, out_shape=[block, block], in_specs=[vmem] + [...  8.35 us

profile of v6, /device:TPU:3, one launch (start us, length us, event | category | flops | bytes accessed | tf_op | source)
XLA Modules:
  0.0 51.0 jit_solution(11590660912830735285)
XLA Ops:
  1.3 41.4 %shard_map.131 = (f32[3,1024,256]{2,1,0:T(8,128)}, f32[3,1024,256]{2,1,0:T(8,128)}, bf16[3,4,32,256]{3,2,1,0:T(8,128)(2,1)}, bf16[2,6,3,16,256]{4,3,2,1,0:T(8,128)(2,1)}, bf16[256,256]{1,0:T(8,128)(2,1)}) custom-call(f32[8]{0:T(128)} %slow_ref.1, f32[8]{0:T(128)} %rigid_ref.1, f32[8]{0:T(128)} %damp_ref.1, s32[32]{0:T(128)} %level_ref.1, ...), custom_call_target="tpu_custom_call" | custom-call | tf_op jit(solution)/shard_map/pallas_call | solution.py:762
  42.7 8.3 %shard_map.132 = (f32[3,1024,256]{2,1,0:T(8,128)}, f32[3,1024,256]{2,1,0:T(8,128)}) custom-call(s32[1,256]{1,0:T(1,128)} %bitcast.15, bf16[2048,256]{1,0:T(8,128)(2,1)} %constant.2.clone.table_hbm, bf16[3,4,32,256]{3,2,1,0:T(8,128)(2,1)} %get-tuple-element.9.half_hbm, bf16[2,6,3,16,256]{4,3,2,1,0:T(8,128)(2,1)} %get-tuple-element.10.side_hbm, ...), custom_call_target="tpu_custom_call" | custom-call | tf_op jit(solution)/shard_map/pallas_call | solution.py:812

commit v7 on v6

--- a/solution.py
+++ b/solution.py
@@ -235,11 +235,20 @@
     for load in loads[:1] + slot_loads + loads[3:] + loads[1:3]:
         load.start()
 
+    def outside(edge, *parts):
+        @pl.when(edge)
+        def _():
+            for part in parts:
+                part[...] = jnp.zeros(part.shape, BF)
+
     for p in range(2):
-        half[p, :, 0:2] = jnp.zeros((3, 2, C, NZ), BF)
-        half[p, :, C + 2 : C + 4] = jnp.zeros((3, 2, C, NZ), BF)
-        for s in range(2):
-            side_in[p, s] = jnp.zeros(side_in.shape[2:], BF)
+        outside(gx == 0, half.at[p, :, 0:2], side_in.at[p, 0, 0], side_in.at[p, 1, 0])
+        outside(
+            gx == GX - 1,
+            half.at[p, :, C + 2 : C + 4], side_in.at[p, 0, TILES + 1], side_in.at[p, 1, TILES + 1],
+        )
+        outside(gy == 0, side_in.at[p, 0])
+        outside(gy == GY - 1, side_in.at[p, 1])
 
     steps = [(1, 0), (-1, 0), (0, 1), (0, -1), (1, 1), (1, -1), (-1, 1), (-1, -1)]
 
@@ -299,28 +308,29 @@
     lax.fori_loop(0, ND, downward, (one, zero), unroll=8)
     zbuf[ND] = zbuf[ND - 1]
 
-    def upward(step, carry):
-        refl_re, refl_im = carry
-        i = ND - 1 - step
-        upper, under = zbuf[i], zbuf[i + 1]
-        r = (upper - under) / (upper + under)
-        leg_re, leg_im = ebuf[0, i], ebuf[1, i]
-        trip_re = leg_re * leg_re - leg_im * leg_im
-        trip_im = 2.0 * leg_re * leg_im
-        upper_re = r + refl_re
-        lower_re = 1.0 + r * refl_re
-        lower_im = r * refl_im
-        scale = 1.0 / (lower_re * lower_re + lower_im * lower_im)
-        ratio_re = (upper_re * lower_re + refl_im * lower_im) * scale
-        ratio_im = (refl_im * lower_re - upper_re * lower_im) * scale
-        fresh_re = trip_re * ratio_re - trip_im * ratio_im
-        fresh_im = trip_re * ratio_im + trip_im * ratio_re
-        down_re, down_im = dbuf[0, i], dbuf[1, i]
-        kbuf[i, :, 0:128] = (down_re * (1.0 + fresh_re) - down_im * fresh_im) * (1.0 / 32.0)
-        kbuf[i, :, 128:256] = (down_re * fresh_im + down_im * (1.0 + fresh_re)) * (1.0 / 32.0)
+    def upward(block_id, carry):
+        top_re, top_im = carry
+        base_re, base_im = one, zero
+        for k in range(8):
+            i = ND - 1 - (8 * block_id + k)
+            upper, under = zbuf[i], zbuf[i + 1]
+            r = (upper - under) / (upper + under)
+            leg_re, leg_im = ebuf[0, i], ebuf[1, i]
+            trip_re = leg_re * leg_re - leg_im * leg_im
+            trip_im = 2.0 * leg_re * leg_im
+            num_re, num_im = r * base_re + top_re, r * base_im + top_im
+            base_re, base_im = base_re + r * top_re, base_im + r * top_im
+            top_re = trip_re * num_re - trip_im * num_im
+            top_im = trip_re * num_im + trip_im * num_re
+            scale = 1.0 / (base_re * base_re + base_im * base_im)
+            fresh_re = (top_re * base_re + top_im * base_im) * scale
+            fresh_im = (top_im * base_re - top_re * base_im) * scale
+            down_re, down_im = dbuf[0, i], dbuf[1, i]
+            kbuf[i, :, 0:128] = (down_re * (1.0 + fresh_re) - down_im * fresh_im) * (1.0 / 32.0)
+            kbuf[i, :, 128:256] = (down_re * fresh_im + down_im * (1.0 + fresh_re)) * (1.0 / 32.0)
         return fresh_re, fresh_im
 
-    lax.fori_loop(0, ND, upward, (zero, zero), unroll=4)
+    lax.fori_loop(0, ND // 8, upward, (zero, zero))
     loads[3].wait()
     product = dot(kbuf[...].reshape(ND * 8, 2 * F).astype(BF), table[AT_WAVES : AT_WAVES + 2 * F])
     product = product[:, :128] + product[:, 128:]

time: 51.2 us -> 51.2 us (level)
  no operation moved by 1% of the time
where the time goes in v7:
time: 51.2 us; the launch traced here: 51 us
  Pallas kernels  49.7 us (97%)
  between operations  1.29 us (3%)
    pallas_call x1, Pallas kernels, shards(): pl.pallas_call(main_kernel, out_shape=[block, block, jax.ShapeDtypeStruct...  41.4 us
    pallas_call x1, Pallas kernels, shards(): pl.pallas_call(last_kernel, out_shape=[block, block], in_specs=[vmem] + [...  8.35 us

profile of v7, /device:TPU:3, one launch (start us, length us, event | category | flops | bytes accessed | tf_op | source)
XLA Modules:
  0.0 51.0 jit_solution(15624787999405554785)
XLA Ops:
  1.3 41.4 %shard_map.131 = (f32[3,1024,256]{2,1,0:T(8,128)}, f32[3,1024,256]{2,1,0:T(8,128)}, bf16[3,4,32,256]{3,2,1,0:T(8,128)(2,1)}, bf16[2,6,3,16,256]{4,3,2,1,0:T(8,128)(2,1)}, bf16[256,256]{1,0:T(8,128)(2,1)}) custom-call(f32[8]{0:T(128)} %slow_ref.1, f32[8]{0:T(128)} %rigid_ref.1, f32[8]{0:T(128)} %damp_ref.1, s32[32]{0:T(128)} %level_ref.1, ...), custom_call_target="tpu_custom_call" | custom-call | tf_op jit(solution)/shard_map/pallas_call | solution.py:772
  42.7 8.3 %shard_map.132 = (f32[3,1024,256]{2,1,0:T(8,128)}, f32[3,1024,256]{2,1,0:T(8,128)}) custom-call(s32[1,256]{1,0:T(1,128)} %bitcast.15, bf16[2048,256]{1,0:T(8,128)(2,1)} %constant.2.clone.table_hbm, bf16[3,4,32,256]{3,2,1,0:T(8,128)(2,1)} %get-tuple-element.9.half_hbm, bf16[2,6,3,16,256]{4,3,2,1,0:T(8,128)(2,1)} %get-tuple-element.10.side_hbm, ...), custom_call_target="tpu_custom_call" | custom-call | tf_op jit(solution)/shard_map/pallas_call | solution.py:822
